TPU v7x, 32 devices: a whole 2x2x4 slice. The times are simulated.
32 devices in a mesh: chain: 2 (over x), pix: 16 (over z, y, core).
Axes of the slice: x: 2, y: 2, z: 4, core: 2. Of those that a mesh axis runs over, the one named last changes fastest.
Arguments:
- latent: float32 [131072, 512], P(('chain', 'pix')), parts along dimension 0, may hold values from -6 to 6
- momentum: float32 [131072, 512], P(('chain', 'pix')), parts along dimension 0, may hold values from -6 to 6
- data: bfloat16 [512, 131072], P('pix', 'chain'), parts along dimension 1, may hold values from -6 to 6
- neighbours: int32 [8, 8], P('chain'), parts along dimension 0, may hold values from -1 to 3, as said below
- spectral_root: bfloat16 [512, 512], replicated, may hold values from -0.125 to 0.125
- log_level: float32 [512], replicated, may hold values from -0.5 to 0.5
- beam_taps: float32 [512, 65, 65], P('pix'), may hold values from -0.09375 to 0.09375
- beam_radius: int32 [512], P('pix'), may hold values from 16 to 32
- noise_weight: float32 [512], P('pix'), may hold values from 0.7 to 12.6
Outputs:
- new_latent: float32 [131072, 512], P(('chain', 'pix')), parts along dimension 0
- new_momentum: float32 [131072, 512], P(('chain', 'pix')), parts along dimension 0
- residual_maps: bfloat16 [512, 131072], P('pix', 'chain'), parts along dimension 1
- misfit: float32 [2], P('chain'), parts along dimension 0
There are 2 independent parts, one for each index of `chain`. A program takes and returns all parts, laid end to end along the dimension named above; an argument that names none is the same for every part. Nothing has to cross between parts.
Inputs may be any that keep to these rules, and one draw needn't show every extreme that they name: The patches tile a 2 x 2 square, each cell holding one patch; neighbours[p, k] is the patch in the cell one step from p's cell in direction k, -1 where that cell lies outside the square.
All inputs are finite; a program needn't handle non-finite values.
Results may differ from a plain program's by a relative error of at most 0.0083.
Values may be sent and summed in bfloat16 or wider, within the bound.
No kernel may reach another device: no remote copies, remote signals or barrier semaphores. Data moves between devices by JAX's collectives and lax.ppermute only.
A program may use at most 192 MiB of HBM per device.

v0:
```python
import math

import jax
import jax.numpy as jnp
from jax import lax
from jax.sharding import PartitionSpec as P

F = 512
S = 128
R = 32
PATCHES = 4
PIXELS = 65536
SPAN = 192
HALF = 97
TAPS = 65


leap_size = 0.25
neighbour_steps = ((-1, -1), (-1, 0), (-1, 1), (0, -1), (0, 1), (1, -1), (1, 0), (1, 1))


def mix(form, left, right):
    return jnp.einsum(form, left, right, preferred_element_type=jnp.float32)


def block_range(step_value, length, reach):
    if step_value < 0:
        return (length - reach, length)
    if step_value > 0:
        return (0, reach)
    return (0, length)


def padded_range(step_value):
    if step_value < 0:
        return (0, R)
    if step_value > 0:
        return (R + S, SPAN)
    return (R, R + S)


def trig_table(count_rows, count_cols):
    row_index = jnp.arange(count_rows, dtype=jnp.int32)[:, None]
    col_index = jnp.arange(count_cols, dtype=jnp.int32)[None, :]
    angle = 2.0 * math.pi / SPAN * (row_index * col_index % SPAN).astype(jnp.float32)
    return (jnp.cos(angle).astype(jnp.bfloat16), jnp.sin(angle).astype(jnp.bfloat16))


def inverse_weights(count_rows):
    row_index = jnp.arange(count_rows, dtype=jnp.int32)[:, None]
    freq_index = jnp.arange(HALF, dtype=jnp.int32)[None, :]
    angle = 2.0 * math.pi / SPAN * (row_index * freq_index % SPAN).astype(jnp.float32)
    edge = (freq_index == 0) | (freq_index == SPAN // 2)
    factor = jnp.where(edge, jnp.float32(1.0), jnp.float32(2.0)) / float(SPAN * SPAN)
    return (
        (factor * jnp.cos(angle)).astype(jnp.bfloat16),
        (factor * jnp.sin(angle)).astype(jnp.bfloat16),
    )


def precise(form, left, right):
    return jnp.einsum(form, left, right, precision=lax.Precision.HIGHEST)


def beam_spectrum(beam_taps, beam_radius):
    offsets = jnp.arange(TAPS, dtype=jnp.int32) - R
    distance = offsets[:, None] * offsets[:, None] + offsets[None, :] * offsets[None, :]
    inside = distance[None, :, :] <= (beam_radius * beam_radius)[:, None, None]
    kernel = jnp.where(inside, beam_taps, jnp.zeros_like(beam_taps))
    freq_rows = jnp.arange(HALF, dtype=jnp.int32)[:, None]
    tap_cols = jnp.arange(TAPS, dtype=jnp.int32)[None, :]
    angle_first = 2.0 * math.pi / SPAN * (freq_rows * tap_cols % SPAN).astype(jnp.float32)
    tap_rows = jnp.arange(TAPS, dtype=jnp.int32)[:, None]
    freq_cols = jnp.arange(SPAN, dtype=jnp.int32)[None, :]
    angle_second = 2.0 * math.pi / SPAN * (tap_rows * freq_cols % SPAN).astype(jnp.float32)
    first_cos = precise("ka,cab->ckb", jnp.cos(angle_first), kernel)
    first_sin = precise("ka,cab->ckb", jnp.sin(angle_first), kernel)
    cos_second = jnp.cos(angle_second)
    sin_second = jnp.sin(angle_second)
    spec_re = precise("ckb,bl->ckl", first_cos, cos_second) - precise(
        "ckb,bl->ckl", first_sin, sin_second
    )
    spec_im = -(
        precise("ckb,bl->ckl", first_cos, sin_second)
        + precise("ckb,bl->ckl", first_sin, cos_second)
    )
    return (spec_re[:, None], spec_im[:, None])


def forward_spectrum(values):
    extent = values.shape[-1]
    cos_rows, sin_rows = trig_table(HALF, extent)
    first_cos = mix("ky,cpyx->cpkx", cos_rows, values).astype(jnp.bfloat16)
    first_sin = mix("ky,cpyx->cpkx", sin_rows, values).astype(jnp.bfloat16)
    cos_cols, sin_cols = trig_table(extent, SPAN)
    part_re = mix("cpkx,xl->cpkl", first_cos, cos_cols) - mix("cpkx,xl->cpkl", first_sin, sin_cols)
    part_im = -(
        mix("cpkx,xl->cpkl", first_cos, sin_cols) + mix("cpkx,xl->cpkl", first_sin, cos_cols)
    )
    return (part_re, part_im)


def back_transform(prod_re, prod_im, extent):
    cos_cols, sin_cols = trig_table(SPAN, extent)
    second_re = (
        mix("cpkl,lx->cpkx", prod_re, cos_cols) - mix("cpkl,lx->cpkx", prod_im, sin_cols)
    ).astype(jnp.bfloat16)
    second_im = (
        mix("cpkl,lx->cpkx", prod_re, sin_cols) + mix("cpkl,lx->cpkx", prod_im, cos_cols)
    ).astype(jnp.bfloat16)
    weight_cos, weight_sin = inverse_weights(extent)
    return mix("yk,cpkx->cpyx", weight_cos, second_re) - mix("yk,cpkx->cpyx", weight_sin, second_im)


def assemble(sky_maps, neighbours):
    patch_ids = jnp.arange(PATCHES, dtype=jnp.int32)
    row_blocks = []
    for row_step in (-1, 0, 1):
        pieces = []
        for col_step in (-1, 0, 1):
            row_first, row_last = block_range(row_step, S, R)
            col_first, col_last = block_range(col_step, S, R)
            source_block = sky_maps[:, :, row_first:row_last, col_first:col_last]
            if row_step == 0 and col_step == 0:
                pieces.append(source_block)
            else:
                direction = neighbour_steps.index((row_step, col_step))
                select = (neighbours[:, direction][:, None] == patch_ids[None, :]).astype(
                    jnp.bfloat16
                )
                pieces.append(mix("pq,cqyx->cpyx", select, source_block).astype(jnp.bfloat16))
        row_blocks.append(jnp.concatenate(pieces, axis=3))
    return jnp.concatenate(row_blocks, axis=2)


def fold_back(grad_padded, neighbours):
    patch_ids = jnp.arange(PATCHES, dtype=jnp.int32)
    grad_total = grad_padded[:, :, R : R + S, R : R + S]
    for direction in range(8):
        row_step, col_step = neighbour_steps[direction]
        pad_row_first, pad_row_last = padded_range(row_step)
        pad_col_first, pad_col_last = padded_range(col_step)
        row_first, row_last = block_range(row_step, S, R)
        col_first, col_last = block_range(col_step, S, R)
        source_block = grad_padded[:, :, pad_row_first:pad_row_last, pad_col_first:pad_col_last]
        select = (neighbours[:, direction][:, None] == patch_ids[None, :]).astype(jnp.float32)
        carried = jnp.einsum("pq,cpyx->cqyx", select, source_block, precision=lax.Precision.HIGHEST)
        grad_total = grad_total + jnp.pad(
            carried, ((0, 0), (0, 0), (row_first, S - row_last), (col_first, S - col_last))
        )
    return grad_total


def shards(
    latent,
    momentum,
    data,
    neighbours,
    spectral_root,
    log_level,
    beam_taps,
    beam_radius,
    noise_weight,
):
    devices = lax.axis_size("pix")
    pix_dev = latent.shape[0]
    chan_dev = data.shape[0]
    latent_low = latent.astype(jnp.bfloat16)
    log_sky = lax.dot_general(
        spectral_root, latent_low, (((1,), (1,)), ((), ())), preferred_element_type=jnp.float32
    )
    sky_flat = lax.all_to_all(
        jnp.exp(log_sky + log_level[:, None]).astype(jnp.bfloat16),
        "pix",
        split_axis=0,
        concat_axis=1,
        tiled=True,
    )
    sky_maps = sky_flat.reshape(chan_dev, PATCHES, S, S)
    spec_re, spec_im = beam_spectrum(beam_taps, beam_radius)
    padded = assemble(sky_maps, neighbours)
    part_re, part_im = forward_spectrum(padded)
    prod_re = (part_re * spec_re + part_im * spec_im).astype(jnp.bfloat16)
    prod_im = (part_im * spec_re - part_re * spec_im).astype(jnp.bfloat16)
    model_map = back_transform(prod_re, prod_im, S)
    residual = model_map - data.reshape(chan_dev, PATCHES, S, S).astype(jnp.float32)
    weight = noise_weight[:, None, None, None]
    partial_sum = 0.5 * jnp.sum(weight * residual * residual)
    misfit = (lax.psum(partial_sum, "pix") / (F * PIXELS)).reshape(1)
    weighted = (weight * residual).astype(jnp.bfloat16)
    grad_re, grad_im = forward_spectrum(weighted)
    back_re = (grad_re * spec_re - grad_im * spec_im).astype(jnp.bfloat16)
    back_im = (grad_re * spec_im + grad_im * spec_re).astype(jnp.bfloat16)
    grad_padded = back_transform(back_re, back_im, SPAN)
    grad_sky = fold_back(grad_padded, neighbours)
    grad_log = (grad_sky * sky_maps.astype(jnp.float32)).astype(jnp.bfloat16)
    grad_blocks = grad_log.reshape(chan_dev, devices, pix_dev)
    grad_latent = lax.dot_general(
        lax.all_to_all(grad_blocks, "pix", split_axis=1, concat_axis=0, tiled=True)[:, 0, :],
        spectral_root,
        (((0,), (0,)), ((), ())),
        preferred_element_type=jnp.float32,
    )
    new_momentum = momentum - leap_size * (latent + grad_latent)
    new_latent = latent + leap_size * new_momentum
    residual_maps = residual.astype(jnp.bfloat16).reshape(chan_dev, devices * pix_dev)
    return (new_latent, new_momentum, residual_maps, misfit)


def solution(mesh):
    placed = (
        P(("chain", "pix"), None),
        P(("chain", "pix"), None),
        P("pix", "chain"),
        P("chain", None),
        P(),
        P(),
        P("pix", None, None),
        P("pix"),
        P("pix"),
    )
    return jax.shard_map(
        shards,
        mesh=mesh,
        in_specs=placed,
        out_specs=(
            P(("chain", "pix"), None),
            P(("chain", "pix"), None),
            P("pix", "chain"),
            P("chain"),
        ),
        check_vma=False,
    )
```

profile of v0, /device:TPU:16, one launch (start us, length us, event | category | flops | bytes accessed | tf_op | source)
XLA Modules:
  0.0 698.3 jit_solution(11181557443143839719)
XLA Ops:
  1.7 7.8 %exponential_convert_fusion = bf16[512,4096]{1,0:T(8,128)(2,1)} fusion(bf16[512,512]{1,0:T(8,128)(2,1)S(1)} %copy-done, f32[512]{0:T(512)} %param.14, f32[4096,512]{1,0:T(8,128)} %param.9), kind=kOutput, calls=%fused_computation.27 | convolution fusion | flops 2153775104 | bytes 13109248 | tf_op jit(solution)/shard_map/dot_general | solution.py:169
  9.5 6.3 all-to-all-start
  19.6 4.9 copy.179
  24.5 9.2 %copy.108 = f32[32,4,128,128]{2,3,1,0:T(8,128)} copy(f32[32,4,128,128]{3,2,1,0:T(8,128)} %bitcast.274) | data formatting | bytes 16777216 | tf_op jit(solution)/shard_map/convert_element_type | solution.py:186
  47.8 5.2 add_negate_fusion.2
  53.0 55.5 %all-to-all-done = bf16[16,32,4096]{2,1,0:T(8,128)(2,1)} async-done(((bf16[16,32,4096]{2,1,0:T(8,128)(2,1)}), bf16[16,32,4096]{2,1,0:T(8,128)(2,1)}, u32[]{:S(2)}, u32[]{:S(2)}) %all-to-all-start) | async-done | bytes 4194336 | tf_op jit(solution)/shard_map/all_to_all | solution.py:172
  108.5 6.5 copy.84
  115.0 7.4 %reshape.87 = bf16[32,4,128,128]{3,2,1,0:T(8,128)(2,1)} reshape(bf16[32,16,4096]{2,1,0:T(8,128)(2,1)} %copy.84) | data formatting | bytes 8388608 | tf_op jit(solution)/shard_map/reshape | solution.py:179
  122.4 5.0 fusion.351
  133.4 6.6 copy.96
  146.7 5.4 copy.104
  161.2 5.2 copy.105
  176.7 19.9 %convolution_convert_fusion.1 = bf16[32,4,192,97]{3,2,1,0:T(8,128)(2,1)} fusion(bf16[32,4,32,192]{2,3,1,0:T(8,128)(2,1)} %copy.105, bf16[32,4,128,32]{2,3,1,0:T(8,128)(2,1)S(1)} %copy.97, bf16[32,4,128,128]{2,3,1,0:T(8,128)(2,1)} %copy.96, bf16[32,4,128,32]{2,3,1,0:T(8,128)(2,1)S(1)} %copy.95, bf16[32,4,32,192]{2,3,1,0:T(8,128)(2,1)} %copy.104), kind=kOutput, calls=%fused_computation.44 | convolution fusion | flops 965162880 | bytes 14204928 | tf_op jit(solution)/shard_map/ky,cpyx->cpkx/dot_general | solution.py:23
  196.6 18.5 %convolution_convert_fusion = bf16[32,4,192,97]{3,2,1,0:T(8,128)(2,1)S(1)} fusion(bf16[32,4,32,192]{2,3,1,0:T(8,128)(2,1)} %copy.105, bf16[32,4,128,32]{2,3,1,0:T(8,128)(2,1)} %copy-done.9, bf16[32,4,128,128]{2,3,1,0:T(8,128)(2,1)S(1)} %copy-done.4, bf16[32,4,128,32]{2,3,1,0:T(8,128)(2,1)S(1)} %copy.95, bf16[32,4,32,192]{2,3,1,0:T(8,128)(2,1)} %copy.104), kind=kOutput, calls=%fused_computation.43 | convolution fusion | flops 965162880 | bytes 14204928 | tf_op jit(solution)/shard_map/ky,cpyx->cpkx/dot_general | solution.py:23
  215.1 7.1 %fusion.11 = f32[32,4,97,192]{2,3,1,0:T(8,128)} fusion(bf16[32,4,192,97]{3,2,1,0:T(8,128)(2,1)S(1)} %convolution_convert_fusion), kind=kOutput, calls=%fused_computation.31 | convolution fusion | flops 915775488 | bytes 14303232 | tf_op jit(solution)/shard_map/cpkx,xl->cpkl/dot_general | solution.py:23
  222.2 7.0 %fusion.13 = f32[32,4,97,192]{2,3,1,0:T(8,128)} fusion(bf16[32,4,192,97]{3,2,1,0:T(8,128)(2,1)S(1)} %convolution_convert_fusion), kind=kOutput, calls=%fused_computation.33 | convolution fusion | flops 915775488 | bytes 14303232 | tf_op jit(solution)/shard_map/cpkx,xl->cpkl/dot_general | solution.py:23
  229.2 7.0 %fusion.15 = f32[32,4,97,192]{2,3,1,0:T(8,128)} fusion(bf16[32,4,192,97]{3,2,1,0:T(8,128)(2,1)S(1)} %bitcast.271), kind=kOutput, calls=%fused_computation.35 | convolution fusion | flops 915775488 | bytes 14303232 | tf_op jit(solution)/shard_map/cpkx,xl->cpkl/dot_general | solution.py:23
  236.2 22.2 %subtract_convert_fusion.2 = (bf16[32,4,97,192]{2,3,1,0:T(8,128)(2,1)}, bf16[32,4,97,192]{2,3,1,0:T(8,128)(2,1)}) fusion(f32[32,97,192]{1,2,0:T(8,128)} %add_negate_fusion.2, f32[32,97,192]{1,2,0:T(8,128)S(1)} %copy-done.3, f32[32,4,97,192]{2,3,1,0:T(8,128)} %fusion.13, f32[32,4,97,192]{2,3,1,0:T(8,128)} %fusion.15, f32[32,4,97,192]{2,3,1,0:T(8,128)} %fusion.11, ...), kind=kOutput, calls=%fused_computation.7 | convolution fusion | flops 941998080 | bytes 47677440 | tf_op jit(solution)/shard_map/cpkx,xl->cpkl/dot_general | solution.py:23
  258.4 8.4 %fusion.152 = f32[32,4,97,128]{3,2,1,0:T(8,128)} fusion(bf16[32,4,97,192]{2,3,1,0:T(8,128)(2,1)} %get-tuple-element.15), kind=kOutput, calls=%fused_computation.192 | convolution fusion | flops 610516992 | bytes 11124736 | tf_op jit(solution)/shard_map/cpkl,lx->cpkx/dot_general | solution.py:23
  266.8 5.4 fusion.146
  272.3 13.1 %fusion.24 = f32[32,4,128,128]{3,2,1,0:T(8,128)} fusion(f32[32,4,97,128]{3,2,1,0:T(8,128)} %fusion.152, bf16[32,4,97,192]{2,3,1,0:T(8,128)(2,1)} %get-tuple-element.14, f32[97]{0:T(128)S(1)} %copy-done.11), kind=kOutput, calls=%fused_computation.45 | convolution fusion | flops 1020679552 | bytes 19513732 | tf_op jit(solution)/shard_map/yk,cpkx->cpyx/dot_general | solution.py:23
  285.4 17.1 %fusion = (f32[]{:T(128)}, bf16[32,4,128,128]{2,3,1,0:T(8,128)(2,1)}, f32[32,4,128,128]{2,3,1,0:T(8,128)}) fusion(f32[32]{0:T(128)S(1)} %copy-done.12, f32[32,4,128,128]{2,3,1,0:T(8,128)} %copy.108, f32[32,4,128,128]{3,2,1,0:T(8,128)} %fusion.24, f32[97]{0:T(128)S(1)} %copy-done.11, f32[32,4,97,128]{3,2,1,0:T(8,128)} %fusion.146, ...), kind=kOutput, calls=%fused_computation.12 | convolution fusion | flops 1033262464 | bytes 40485384 | tf_op jit(solution)/shard_map/yk,cpkx->cpyx/dot_general | solution.py:23
  302.5 6.2 convolution_convert_fusion.2
  308.8 7.5 %fusion.26 = f32[32,4,97,192]{2,3,1,0:T(8,128)} fusion(bf16[32,4,128,97]{2,3,1,0:T(8,128)(2,1)S(1)} %convolution_convert_fusion.2), kind=kOutput, calls=%fused_computation.47 | convolution fusion | flops 610516992 | bytes 12713984 | tf_op jit(solution)/shard_map/cpkx,xl->cpkl/dot_general | solution.py:23
  316.3 7.4 %fusion.28 = f32[32,4,97,192]{2,3,1,0:T(8,128)} fusion(bf16[32,4,128,97]{2,3,1,0:T(8,128)(2,1)S(1)} %convolution_convert_fusion.2), kind=kOutput, calls=%fused_computation.49 | convolution fusion | flops 610516992 | bytes 12713984 | tf_op jit(solution)/shard_map/cpkx,xl->cpkl/dot_general | solution.py:23
  328.3 7.4 %fusion.30 = f32[32,4,97,192]{2,3,1,0:T(8,128)} fusion(bf16[32,4,128,97]{2,3,1,0:T(8,128)(2,1)S(1)} %convolution_convert_fusion.3), kind=kOutput, calls=%fused_computation.51 | convolution fusion | flops 610516992 | bytes 12713984 | tf_op jit(solution)/shard_map/cpkx,xl->cpkl/dot_general | solution.py:23
  335.7 20.3 %add_convert_fusion.1 = (bf16[32,4,97,192]{2,3,1,0:T(8,128)(2,1)}, bf16[32,4,97,192]{2,3,1,0:T(8,128)(2,1)S(1)}) fusion(f32[32,97,192]{1,2,0:T(8,128)} %add_negate_fusion.2, f32[32,97,192]{1,2,0:T(8,128)} %convolution_subtract_fusion, f32[32,4,97,192]{2,3,1,0:T(8,128)} %fusion.28, f32[32,4,97,192]{2,3,1,0:T(8,128)} %fusion.30, ...), kind=kOutput, calls=%fused_computation.4 | convolution fusion | flops 636739584 | bytes 46088192 | tf_op jit(solution)/shard_map/cpkx,xl->cpkl/dot_general | solution.py:23
  355.9 7.0 fusion.85
  362.9 7.1 %fusion.77 = f32[32,4,97,192]{2,3,1,0:T(8,128)} fusion(bf16[32,4,97,192]{2,3,1,0:T(8,128)(2,1)S(1)} %get-tuple-element.13), kind=kOutput, calls=%fused_computation.134 | convolution fusion | flops 915775488 | bytes 14303232 | tf_op jit(solution)/shard_map/cpkl,lx->cpkx/dot_general | solution.py:23
  370.0 15.3 %fusion.10 = f32[32,4,192,192]{3,2,1,0:T(8,128)} fusion(f32[32,4,97,192]{2,3,1,0:T(8,128)} %fusion.85, bf16[32,4,97,192]{2,3,1,0:T(8,128)(2,1)} %get-tuple-element.12, f32[97]{0:T(128)S(1)} %copy-done.11), kind=kOutput, calls=%fused_computation.30 | convolution fusion | flops 1836154880 | bytes 33177988 | tf_op jit(solution)/shard_map/yk,cpkx->cpyx/dot_general | solution.py:23
  385.3 25.5 %subtract_bitcast_fusion = f32[32,4,192,192]{2,3,1,0:T(8,128)} fusion(f32[32,4,192,192]{3,2,1,0:T(8,128)} %fusion.10, f32[32,4,97,192]{2,3,1,0:T(8,128)} %fusion.77, bf16[32,4,97,192]{2,3,1,0:T(8,128)(2,1)} %get-tuple-element.12, f32[97]{0:T(128)S(1)} %copy-done.11), kind=kOutput, calls=%fused_computation | convolution fusion | flops 1840873472 | bytes 52052356 | tf_op jit(solution)/shard_map/yk,cpkx->cpyx/dot_general | solution.py:23
  415.4 11.6 %fusion.349 = (f32[32,4,32,128]{2,3,1,0:T(8,128)}, f32[32,4,32,128]{2,3,1,0:T(8,128)}) fusion(f32[32,4,192,192]{2,3,1,0:T(8,128)} %subtract_bitcast_fusion), kind=kLoop, calls=%fused_computation.362 | loop fusion | bytes 8388608 | tf_op jit(solution)/shard_map/slice | solution.py:145
  427.0 8.1 %fusion.348 = (f32[32,4,32,32]{2,3,1,0:T(8,128)}, f32[32,4,32,32]{2,3,1,0:T(8,128)}, f32[32,4,32,32]{2,3,1,0:T(8,128)}, f32[32,4,32,32]{2,3,1,0:T(8,128)}) fusion(f32[32,4,192,192]{2,3,1,0:T(8,128)} %subtract_bitcast_fusion), kind=kLoop, calls=%fused_computation.361 | loop fusion | bytes 4194304 | tf_op jit(solution)/shard_map/slice | solution.py:145
  444.2 5.2 copy.113
  453.0 6.2 copy.114
  459.3 5.4 copy.123
  468.2 6.2 copy.124
  484.9 5.1 fusion.232
  495.8 5.1 fusion.225
  507.0 5.1 fusion.219
  519.7 15.1 %fusion.9 = bf16[32,4,128,128]{2,3,1,0:T(8,128)(2,1)} fusion(f32[32,4,192,192]{2,3,1,0:T(8,128)} %subtract_bitcast_fusion, bf16[32,4,128,128]{2,3,1,0:T(8,128)(2,1)S(1)} %copy-done.5, f32[32,4,32,32]{2,3,1,0:T(8,128)} %bitcast.279, f32[32,4,32,128]{2,3,1,0:T(8,128)} %bitcast.273, f32[32,4,32,32]{2,3,1,0:T(8,128)S(1)} %bitcast.278, ...), kind=kLoop, calls=%fused_computation.22 | loop fusion | flops 23068672 | bytes 27262976 | tf_op jit(solution)/shard_map/convert_element_type | solution.py:196
  534.8 6.4 copy.128
  541.2 7.3 %reshape.88 = bf16[32,16,4096]{2,1,0:T(8,128)(2,1)} reshape(bf16[32,4,128,128]{3,2,1,0:T(8,128)(2,1)} %copy.128) | data formatting | bytes 8388608 | tf_op jit(solution)/shard_map/reshape | solution.py:197
  548.4 6.5 copy.129
  560.3 110.6 %psum.7 = f32[]{:T(128)} all-reduce(f32[]{:T(128)S(6)} %mul_shard_map.3), channel_id=1, replica_groups=mesh['chain'=2,'pix'=16] {'pix'}, use_global_device_ids=true, to_apply=%region_1.2 | all-reduce | flops 1 | bytes 8 | tf_op jit(solution)/shard_map/psum | solution.py:189
  670.9 6.4 copy.130
  677.3 6.9 copy.200
  684.9 12.0 %multiply_add_fusion = (f32[4096,512]{1,0:T(8,128)}, f32[4096,512]{1,0:T(8,128)}) fusion(f32[4096,512]{1,0:T(8,128)} %param.9, f32[4096,512]{1,0:T(8,128)} %param.10, bf16[512,4096]{1,0:T(8,128)(2,1)} %bitcast.90, bf16[512,512]{1,0:T(8,128)(2,1)S(1)} %copy-done), kind=kOutput, calls=%fused_computation.25 | convolution fusion | flops 2157969408 | bytes 38273024 | tf_op jit(solution)/shard_map/dot_general | solution.py:198
  (122 shorter events, 111.0 us)
Async XLA Ops:
  0.6 1.0 copy-start
  9.5 6.3 copy-start.29
  9.5 6.4 copy-start.8
  9.5 99.0 %all-to-all-start = ((bf16[16,32,4096]{2,1,0:T(8,128)(2,1)}), bf16[16,32,4096]{2,1,0:T(8,128)(2,1)}, u32[]{:S(2)}, u32[]{:S(2)}) async-start(bf16[16,32,4096]{2,1,0:T(8,128)(2,1)} %bitcast.280), calls=%async_computation | async-start | bytes 8388608 | tf_op jit(solution)/shard_map/all_to_all | solution.py:172
  24.5 9.7 %copy-start.10 = (s32[4,8]{1,0:T(4,128)S(1)}, s32[4,8]{1,0:T(4,128)}, u32[]{:S(2)}) copy-start(s32[4,8]{1,0:T(4,128)} %param.12) | copy-start | bytes 388
  34.5 105.5 %copy-start.23 = (s32[4]{0:T(128)}, s32[4]{0:T(128)S(1)}, u32[]{:S(2)}) copy-start(s32[4]{0:T(128)S(1)} %get-tuple-element.4) | copy-start | bytes 52
  34.5 107.5 %copy-start.21 = (s32[4]{0:T(128)}, s32[4]{0:T(128)S(1)}, u32[]{:S(2)}) copy-start(s32[4]{0:T(128)S(1)} %get-tuple-element.8) | copy-start | bytes 52
  34.5 108.3 %copy-start.27 = (s32[4]{0:T(128)}, s32[4]{0:T(128)S(1)}, u32[]{:S(2)}) copy-start(s32[4]{0:T(128)S(1)} %get-tuple-element.9) | copy-start | bytes 52
  34.5 117.6 %copy-start.19 = (s32[4]{0:T(128)}, s32[4]{0:T(128)S(1)}, u32[]{:S(2)}) copy-start(s32[4]{0:T(128)S(1)} %get-tuple-element.5) | copy-start | bytes 52
  34.5 119.6 %copy-start.17 = (s32[4]{0:T(128)}, s32[4]{0:T(128)S(1)}, u32[]{:S(2)}) copy-start(s32[4]{0:T(128)S(1)} %get-tuple-element.10) | copy-start | bytes 52
  34.5 121.6 %copy-start.25 = (s32[4]{0:T(128)}, s32[4]{0:T(128)S(1)}, u32[]{:S(2)}) copy-start(s32[4]{0:T(128)S(1)} %get-tuple-element.11) | copy-start | bytes 52
  34.6 135.5 %copy-start.13 = (s32[4]{0:T(128)}, s32[4]{0:T(128)S(1)}, u32[]{:S(2)}) copy-start(s32[4]{0:T(128)S(1)} %get-tuple-element.7) | copy-start | bytes 52
  34.6 140.2 %copy-start.15 = (s32[4]{0:T(128)}, s32[4]{0:T(128)S(1)}, u32[]{:S(2)}) copy-start(s32[4]{0:T(128)S(1)} %get-tuple-element.6) | copy-start | bytes 52
  122.4 5.0 copy-start.1
  175.7 1.0 copy-start.9
  176.7 19.9 %copy-start.4 = (bf16[32,4,128,128]{2,3,1,0:T(8,128)(2,1)S(1)}, bf16[32,4,128,128]{2,3,1,0:T(8,128)(2,1)}, u32[]{:S(2)}) copy-start(bf16[32,4,128,128]{2,3,1,0:T(8,128)(2,1)} %copy.96) | copy-start | bytes 12582916
  215.1 14.1 %slice-start.4 = ((s8[6291456]{0:T(1024)(128)(4,1)}), s8[4194304]{0:T(1024)(128)(4,1)S(1)}, s32[]{:S(2)}) async-start(s8[6291456]{0:T(1024)(128)(4,1)} %bitcast.270), calls=%async_computation.6 | async-start | bytes 8388608
  222.2 7.0 %slice-start.5 = ((s8[6291456]{0:T(1024)(128)(4,1)}), s8[2097152]{0:T(1024)(128)(4,1)S(1)}, s32[]{:S(2)}) async-start(s8[6291456]{0:T(1024)(128)(4,1)} %bitcast.270), calls=%async_computation.7 | async-start | bytes 4194304
  229.2 7.0 %copy-start.3 = (f32[32,97,192]{1,2,0:T(8,128)S(1)}, f32[32,97,192]{1,2,0:T(8,128)}, u32[]{:S(2)}) copy-start(f32[32,97,192]{1,2,0:T(8,128)} %convolution_subtract_fusion) | copy-start | bytes 7151620
  258.4 8.4 %slice-start = ((s8[6291456]{0:T(1024)(128)(4,1)}), s8[4194304]{0:T(1024)(128)(4,1)S(1)}, s32[]{:S(2)}) async-start(s8[6291456]{0:T(1024)(128)(4,1)} %bitcast.266), calls=%async_computation.2 | async-start | bytes 8388608
  258.4 8.4 %slice-start.1 = ((s8[6291456]{0:T(1024)(128)(4,1)}), s8[2097152]{0:T(1024)(128)(4,1)S(1)}, s32[]{:S(2)}) async-start(s8[6291456]{0:T(1024)(128)(4,1)} %bitcast.266), calls=%async_computation.3 | async-start | bytes 4194304
  266.8 5.4 copy-start.11
  272.3 13.1 %copy-start.12 = (f32[32]{0:T(128)S(1)}, f32[32]{0:T(128)}, u32[]{:S(2)}) copy-start(f32[32]{0:T(128)} %param.17) | copy-start | bytes 388
  308.8 14.9 %slice-start.2 = ((s8[8388608]{0:T(1024)(128)(4,1)}), s8[4194304]{0:T(1024)(128)(4,1)S(1)}, s32[]{:S(2)}) async-start(s8[8388608]{0:T(1024)(128)(4,1)} %bitcast.268), calls=%async_computation.4 | async-start | bytes 8388608
  316.3 7.4 %slice-start.3 = ((s8[8388608]{0:T(1024)(128)(4,1)}), s8[4194304]{0:T(1024)(128)(4,1)S(1)}, s32[]{:S(2)}) async-start(s8[8388608]{0:T(1024)(128)(4,1)} %bitcast.268), calls=%async_computation.5 | async-start | bytes 8388608
  326.5 1.8 copy-start.2
  427.0 8.1 %copy-start.16 = (s32[4]{0:T(128)S(1)}, s32[4]{0:T(128)}, u32[]{:S(2)}) copy-start(s32[4]{0:T(128)} %copy-done.15) | copy-start | bytes 52
  427.0 12.6 %copy-start.14 = (s32[4]{0:T(128)S(1)}, s32[4]{0:T(128)}, u32[]{:S(2)}) copy-start(s32[4]{0:T(128)} %copy-done.13) | copy-start | bytes 52
  444.2 5.2 copy-start.28
  459.3 5.4 copy-start.26
  468.2 8.3 %copy-start.24 = (s32[4]{0:T(128)S(1)}, s32[4]{0:T(128)}, u32[]{:S(2)}) copy-start(s32[4]{0:T(128)} %copy-done.23) | copy-start | bytes 52
  476.5 8.4 %copy-start.22 = (s32[4]{0:T(128)S(1)}, s32[4]{0:T(128)}, u32[]{:S(2)}) copy-start(s32[4]{0:T(128)} %copy-done.21) | copy-start | bytes 52
  484.9 10.9 %copy-start.20 = (s32[4]{0:T(128)S(1)}, s32[4]{0:T(128)}, u32[]{:S(2)}) copy-start(s32[4]{0:T(128)} %copy-done.19) | copy-start | bytes 52
  495.8 11.1 %copy-start.18 = (s32[4]{0:T(128)S(1)}, s32[4]{0:T(128)}, u32[]{:S(2)}) copy-start(s32[4]{0:T(128)} %copy-done.17) | copy-start | bytes 52
  514.9 3.4 copy-start.5
  514.9 4.1 copy-start.6
  514.9 4.7 copy-start.7
  554.9 130.0 %all-to-all-start.1 = ((bf16[32,16,4096]{2,0,1:T(8,128)(2,1)}), bf16[32,16,4096]{2,0,1:T(8,128)(2,1)}, u32[]{:S(2)}, u32[]{:S(2)}) async-start(bf16[32,16,4096]{2,0,1:T(8,128)(2,1)} %copy.129), calls=%async_computation.1 | async-start | bytes 8388608 | tf_op jit(solution)/shard_map/all_to_all | solution.py:199
where the time goes:
time: 705 us; the launch traced here: 698 us
  matrix products  317 us (45%)
  local copies, waits for them, and re-layouts  176 us (25%)
  blocking collectives  111 us (16%)
  waiting for transfers between devices  55.5 us (8%)
  other arithmetic  24.9 us (4%)
  starting transfers between devices  11 us (2%)
    dot_general x28, matrix products, mix(): return jnp.einsum(form, left, right, preferred_element_type=jnp.float32)  243 us
    psum x1, blocking collectives, shards(): misfit = (lax.psum(partial_sum, 'pix') / (F * PIXELS)).reshape(1)  111 us
    all_to_all x1, waiting for transfers between devices, shards(): lax.all_to_all(jnp.exp(log_sky + log_level[:, None]).astype(jnp.bfloat16)...  55.5 us
    slice x9, local copies, waits for them, and re-layouts, fold_back(): grad_padded[:, :, pad_row_first:pad_row_last, pad_col_first:pad_col_last]  45.7 us
    dot_general x8, matrix products, fold_back(): jnp.einsum('pq,cpyx->cqyx', select, source_block, precision=lax.Precision...  35.1 us
    unnamed x76, local copies, waits for them, and re-layouts  24.8 us
    dot_general x6, local copies, waits for them, and re-layouts, fold_back(): jnp.einsum('pq,cpyx->cqyx', select, source_block, precision=lax.Precision...  23.1 us
    dot_general x6, matrix products, precise(): return jnp.einsum(form, left, right, precision=lax.Precision.HIGHEST)  18.4 us
  transfers between devices with their start and end apart: 2, of which 1 were waited for; matrix products, arithmetic and copies ran while one was open for 7% of the time, Pallas kernels for 0%

commit v1 on v0

v1 whole, which is shorter than its diff:
```python
import functools
import math

import jax
import jax.numpy as jnp
import numpy as np
from jax import lax
from jax.experimental import pallas as pl
from jax.experimental.pallas import tpu as pltpu
from jax.sharding import PartitionSpec as P

S = 128
R = 32
PATCHES = 4
TAPS = 65
SIDE = 2 * S
SPAN = SIDE + R
HALF = SPAN // 2
LANES = 256
TAP_ROWS = 80
TAP_LANES = 128
BLOCK = 16

leap_size = 0.25


def half_tables(positions):
    angle = 2.0 * math.pi / SPAN * (np.arange(HALF)[:, None] + 0.5) * positions[None, :]
    return np.cos(angle), np.sin(angle)


def tables():
    low = jnp.bfloat16
    cos_image, sin_image = half_tables(np.arange(SIDE))
    cos_taps, sin_taps = half_tables(np.arange(TAPS) - R)
    rows = np.concatenate([cos_image, sin_image], axis=0)
    cols = np.zeros((2 * LANES, SIDE))
    cols[:HALF] = cos_image
    cols[LANES : LANES + HALF] = sin_image
    tap_rows = np.zeros((SPAN, TAP_ROWS))
    tap_rows[:, :TAPS] = np.concatenate([cos_taps, sin_taps], axis=0)
    tap_cols = np.zeros((TAP_LANES, 2 * LANES))
    tap_cols[:TAPS, :HALF] = cos_taps.T
    tap_cols[:TAPS, LANES : LANES + HALF] = sin_taps.T
    return (
        np.asarray(rows, low),
        np.asarray(rows.T, low),
        np.asarray(cols, low),
        np.asarray(cols.T, low),
        np.asarray(np.concatenate([tap_rows, tap_rows], axis=1), low),
        np.asarray(np.concatenate([tap_cols, tap_cols], axis=0), low),
    )


def dot(left, right):
    return lax.dot_general(
        left, right, (((1,), (0,)), ((), ())), preferred_element_type=jnp.float32
    )


def split_low(values):
    high = values.astype(jnp.bfloat16)
    return high, (values - high.astype(jnp.float32)).astype(jnp.bfloat16)


def convolve_kernel(
    strip_rows,
    order_ref,
    noise_ref,
    sky_ref,
    data_ref,
    taps_ref,
    rows_ref,
    rows_t_ref,
    cols_ref,
    cols_t_ref,
    tap_rows_ref,
    tap_cols_ref,
    residual_ref,
    grad_ref,
    misfit_ref,
    image_ref,
    data_image_ref,
):
    strips = S // strip_rows
    channels = sky_ref.shape[1]

    def strip_loop(body):
        def step(index, carry):
            cell = index // strips
            strip = index % strips
            cell_row, cell_col = cell // 2, cell % 2
            patch = order_ref[cell]
            device = patch * strips + strip
            base = cell_row * S + strip * strip_rows
            pixel_base = device * (strip_rows * S)
            for row in range(strip_rows):
                body(
                    cell_col,
                    device,
                    row,
                    pl.ds(base + row, channels, stride=SIDE),
                    pl.ds(pl.multiple_of(pixel_base + row * S, S), S),
                )
            return carry

        lax.fori_loop(0, PATCHES * strips, step, 0)

    def spread(cell_col, device, row, spread_rows, pixels):
        lanes = pl.ds(row * S, S)
        image_ref[cell_col, spread_rows, :] = sky_ref[device, :, lanes].astype(jnp.float32)
        data_image_ref[cell_col, spread_rows, :] = data_ref[:, pixels].astype(jnp.float32)

    def gather(cell_col, device, row, spread_rows, pixels):
        lanes = pl.ds(row * S, S)
        grad_ref[device, :, lanes] = image_ref[cell_col, spread_rows, :].astype(jnp.bfloat16)
        residual_ref[:, pixels] = data_image_ref[cell_col, spread_rows, :].astype(jnp.bfloat16)

    def quarters(values):
        return (
            values[:HALF, :LANES],
            values[:HALF, LANES:],
            values[HALF:, :LANES],
            values[HALF:, LANES:],
        )

    def signed_pair(values):
        cc, cs, sc, ss = quarters(values)
        return cc - ss, sc + cs, cc + ss, sc - cs

    def filter_image(image, beam, conjugate):
        first = dot(rows_ref[...], image).astype(jnp.bfloat16)
        re_plus, im_plus, re_minus, im_minus = signed_pair(dot(first, cols_t_ref[...]))
        beam_re_plus, beam_im_plus, beam_re_minus, beam_im_minus = beam
        if conjugate:
            out_re_plus = re_plus * beam_re_plus + im_plus * beam_im_plus
            out_im_plus = im_plus * beam_re_plus - re_plus * beam_im_plus
            out_re_minus = re_minus * beam_re_minus + im_minus * beam_im_minus
            out_im_minus = im_minus * beam_re_minus - re_minus * beam_im_minus
        else:
            out_re_plus = re_plus * beam_re_plus - im_plus * beam_im_plus
            out_im_plus = im_plus * beam_re_plus + re_plus * beam_im_plus
            out_re_minus = re_minus * beam_re_minus - im_minus * beam_im_minus
            out_im_minus = im_minus * beam_re_minus + re_minus * beam_im_minus
        product = jnp.concatenate(
            [
                jnp.concatenate([out_re_plus + out_re_minus, out_im_plus - out_im_minus], axis=1),
                jnp.concatenate([out_im_plus + out_im_minus, out_re_minus - out_re_plus], axis=1),
            ],
            axis=0,
        ).astype(jnp.bfloat16)
        second = dot(product, cols_ref[...]).astype(jnp.bfloat16)
        return dot(rows_t_ref[...], second)

    def channel_step(channel, carry):
        here = pl.ds(pl.multiple_of(channel * SIDE, SIDE), SIDE)
        tap_high, tap_low = split_low(taps_ref[channel])
        tap_first = dot(tap_rows_ref[...], jnp.concatenate([tap_high, tap_low], axis=0))
        first_high, first_low = split_low(tap_first * (2.0 / (SPAN * SPAN)))
        spectrum = dot(jnp.concatenate([first_high, first_low], axis=1), tap_cols_ref[...])
        beam = signed_pair(spectrum)
        image = jnp.concatenate([image_ref[0, here, :], image_ref[1, here, :]], axis=1)
        model = filter_image(image.astype(jnp.bfloat16), beam, True)
        data = jnp.concatenate([data_image_ref[0, here, :], data_image_ref[1, here, :]], axis=1)
        residual = model - data
        data_image_ref[0, here, :] = residual[:, :S]
        data_image_ref[1, here, :] = residual[:, S:]
        weighted = noise_ref[channel] * residual
        misfit_ref[...] += jnp.sum((weighted * residual).reshape(SIDE // 8, 8, SIDE), axis=0)
        grad = filter_image(weighted.astype(jnp.bfloat16), beam, False) * image
        image_ref[0, here, :] = grad[:, :S]
        image_ref[1, here, :] = grad[:, S:]
        return carry

    misfit_ref[...] = jnp.zeros_like(misfit_ref)
    strip_loop(spread)
    lax.fori_loop(0, channels, channel_step, 0)
    strip_loop(gather)


def convolve(order, noise_weight, sky, data, taps):
    devices, channels, strip = sky.shape
    smem = pl.BlockSpec(memory_space=pltpu.SMEM)
    vmem = pl.BlockSpec(memory_space=pltpu.VMEM)
    constants = tables()
    pixels = devices * strip
    macs = channels * (2 * 1952 + 1440) * 256 * 256
    return pl.pallas_call(
        functools.partial(convolve_kernel, strip // S),
        out_shape=(
            jax.ShapeDtypeStruct((channels, pixels), jnp.bfloat16),
            jax.ShapeDtypeStruct(sky.shape, jnp.bfloat16),
            jax.ShapeDtypeStruct((8, SIDE), jnp.float32),
        ),
        in_specs=[smem, smem] + [vmem] * (3 + len(constants)),
        out_specs=(vmem, vmem, vmem),
        scratch_shapes=[
            pltpu.VMEM((2, channels * SIDE, S), jnp.float32),
            pltpu.VMEM((2, channels * SIDE, S), jnp.float32),
        ],
        compiler_params=pltpu.CompilerParams(vmem_limit_bytes=44 * 1024 * 1024),
        cost_estimate=pl.CostEstimate(
            flops=2 * macs, bytes_accessed=8 * channels * pixels, transcendentals=0
        ),
    )(order, noise_weight, sky, data, taps, *constants)


def cell_order(neighbours):
    has_above = neighbours[:, 1] != -1
    has_left = neighbours[:, 3] != -1
    cells = 2 * has_above.astype(jnp.int32) + has_left.astype(jnp.int32)
    patch_ids = jnp.arange(PATCHES, dtype=jnp.int32)
    match = cells[None, :] == patch_ids[:, None]
    return jnp.sum(jnp.where(match, patch_ids[None, :], 0), axis=1)


def masked_taps(beam_taps, beam_radius):
    offsets = jnp.arange(TAPS, dtype=jnp.int32) - R
    distance = offsets[:, None] * offsets[:, None] + offsets[None, :] * offsets[None, :]
    inside = distance[None, :, :] <= (beam_radius * beam_radius)[:, None, None]
    kernel = jnp.where(inside, beam_taps, jnp.zeros_like(beam_taps))
    return jnp.pad(kernel, ((0, 0), (0, TAP_ROWS - TAPS), (0, TAP_LANES - TAPS)))


def shards(
    latent,
    momentum,
    data,
    neighbours,
    spectral_root,
    log_level,
    beam_taps,
    beam_radius,
    noise_weight,
):
    devices = lax.axis_size("pix")
    pix_dev = latent.shape[0]
    chan_dev = data.shape[0]
    freqs = spectral_root.shape[0]
    chunks = chan_dev // BLOCK
    latent_low = latent.astype(jnp.bfloat16)
    root_parts = spectral_root.reshape(devices, chunks, BLOCK, freqs)
    level_parts = log_level.reshape(devices, chunks, BLOCK)
    order = cell_order(neighbours)
    taps = masked_taps(beam_taps, beam_radius)

    skies = []
    for chunk in range(chunks):
        root = root_parts[:, chunk].reshape(devices * BLOCK, freqs)
        level = level_parts[:, chunk].reshape(devices * BLOCK)
        log_sky = lax.dot_general(
            root, latent_low, (((1,), (1,)), ((), ())), preferred_element_type=jnp.float32
        )
        sky = jnp.exp(log_sky + level[:, None]).astype(jnp.bfloat16)
        skies.append(sky.reshape(devices, BLOCK, pix_dev))

    residuals, partials, grads = [], [], []
    for chunk in range(chunks):
        here = slice(chunk * BLOCK, (chunk + 1) * BLOCK)
        sky = lax.all_to_all(skies[chunk], "pix", split_axis=0, concat_axis=0, tiled=True)
        residual, grad, partial = convolve(order, noise_weight[here], sky, data[here], taps[here])
        residuals.append(residual)
        partials.append(jnp.sum(partial))
        grads.append(lax.all_to_all(grad, "pix", split_axis=0, concat_axis=0, tiled=True))

    misfit = (0.5 * lax.psum(sum(partials), "pix") / (freqs * devices * pix_dev)).reshape(1)
    grad_latent = 0.0
    for chunk in range(chunks):
        grad_latent = grad_latent + lax.dot_general(
            grads[chunk].reshape(devices * BLOCK, pix_dev),
            root_parts[:, chunk].reshape(devices * BLOCK, freqs),
            (((0,), (0,)), ((), ())),
            preferred_element_type=jnp.float32,
        )
    new_momentum = momentum - leap_size * (latent + grad_latent)
    new_latent = latent + leap_size * new_momentum
    residual_maps = jnp.concatenate(residuals, axis=0)
    return (new_latent, new_momentum, residual_maps, misfit)


def solution(mesh):
    placed = (
        P(("chain", "pix"), None),
        P(("chain", "pix"), None),
        P("pix", "chain"),
        P("chain", None),
        P(),
        P(),
        P("pix", None, None),
        P("pix"),
        P("pix"),
    )
    return jax.shard_map(
        shards,
        mesh=mesh,
        in_specs=placed,
        out_specs=(
            P(("chain", "pix"), None),
            P(("chain", "pix"), None),
            P("pix", "chain"),
            P("chain"),
        ),
        check_vma=False,
    )
```

time: 705 us -> 277 us (0.39)
  matrix products: 317 us -> 32.4 us
  local copies, waits for them, and re-layouts: 176 us -> 17.6 us
  Pallas kernels: 0 us -> 89.2 us
  blocking collectives: 111 us -> 62.3 us
  other arithmetic: 24.9 us -> 6.19 us
  waiting for transfers between devices: 55.5 us -> 41.6 us
  starting transfers between devices: 11 us -> 22.9 us
    dot_general x44 -> x4, matrix products: 317 us -> 32.4 us  [the longest x2 20.2 us: shards(): lax.dot_general(grads[chunk].reshape(devices * BLOCK, pix_dev), root_part...]
    pallas_call x0 -> x2, Pallas kernels: none -> 89.2 us  [convolve(): pl.pallas_call(functools.partial(convolve_kernel, strip // S), out_shape=...]
    slice x13 -> x5, local copies, waits for them, and re-layouts: 57.1 us -> 5.18 us  [the longest x1 3.9 us: shards(): data[here]]
    psum x1, blocking collectives: 111 us -> 62.3 us  [shards(): lax.psum(sum(partials), 'pix')]
    reshape x4 -> x1, local copies, waits for them, and re-layouts: 27.7 us -> 0.77 us  [shards(): level_parts = log_level.reshape(devices, chunks, BLOCK)]
    dot_general x6 -> x0, local copies, waits for them, and re-layouts: 23.1 us -> none  [fold_back(): jnp.einsum('pq,cpyx->cqyx', select, source_block, precision=lax.Precision...]
    convert_element_type x5 -> x0, local copies, waits for them, and re-layouts: 22.4 us -> none  [the longest x1 9.15 us: shards(): data.reshape(chan_dev, PATCHES, S, S).astype(jnp.float32)]
    convert_element_type x1 -> x0, other arithmetic: 15.1 us -> none  [shards(): grad_log = (grad_sky * sky_maps.astype(jnp.float32)).astype(jnp.bfloat16)]
  transfers between devices with their start and end apart: 2 -> 4, of which waited for: 1 -> 1; matrix products, arithmetic and copies ran while one was open for 7% -> 8% of each run, Pallas kernels for 0% -> 32%
where the time goes in v1:
time: 277 us; the launch traced here: 276 us
  Pallas kernels  89.2 us (32%)
  blocking collectives  62.3 us (22%)
  waiting for transfers between devices  41.6 us (15%)
  matrix products  32.4 us (12%)
  starting transfers between devices  22.9 us (8%)
  local copies, waits for them, and re-layouts  17.6 us (6%)
  other arithmetic  6.19 us (2%)
  between operations  3.91 us (1%)
    pallas_call x2, Pallas kernels, convolve(): pl.pallas_call(functools.partial(convolve_kernel, strip // S), out_shape=...  89.2 us
    psum x1, blocking collectives, shards(): lax.psum(sum(partials), 'pix')  62.3 us
    all_to_all x2, waiting for transfers between devices, shards(): lax.all_to_all(skies[chunk], 'pix', split_axis=0, concat_axis=0, tiled=True)  41.6 us
    dot_general x2, matrix products, shards(): lax.dot_general(grads[chunk].reshape(devices * BLOCK, pix_dev), root_part...  20.2 us
    dot_general x2, matrix products, shards(): lax.dot_general(root, latent_low, (((1,), (1,)), ((), ())), preferred_ele...  12.2 us
    all_to_all x2, starting transfers between devices, shards(): lax.all_to_all(grad, 'pix', split_axis=0, concat_axis=0, tiled=True)  12.1 us
    unnamed x50, local copies, waits for them, and re-layouts  11.5 us
    all_to_all x2, starting transfers between devices, shards(): lax.all_to_all(skies[chunk], 'pix', split_axis=0, concat_axis=0, tiled=True)  10.9 us
  transfers between devices with their start and end apart: 4, of which 1 were waited for; matrix products, arithmetic and copies ran while one was open for 8% of the time, Pallas kernels for 32%

profile of v1, /device:TPU:16, one launch (start us, length us, event | category | flops | bytes accessed | tf_op | source)
XLA Modules:
  0.0 276.2 jit_solution(8057609235198269948)
XLA Ops:
  0.6 0.8 reshape.94
  1.5 0.1 add.74
  1.5 1.1 fusion.7
  2.6 6.2 %fusion.2 = bf16[256,4096]{1,0:T(8,128)(2,1)} fusion(bf16[256,512]{1,0:T(8,128)(2,1)S(1)} %bitcast.18, f32[256]{0:T(256)S(1)} %add.74, f32[4096,512]{1,0:T(8,128)} %param.21), kind=kOutput, calls=%fused_computation.6 | convolution fusion | flops 1077936128 | bytes 10748928 | tf_op jit(solution)/shard_map/dot_general | solution.py:251
  8.8 6.2 %all-to-all-start = ((bf16[16,16,4096]{2,1,0:T(8,128)(2,1)}), bf16[16,16,4096]{2,1,0:T(8,128)(2,1)S(1)}, u32[]{:S(2)}, u32[]{:S(2)}) async-start(bf16[16,16,4096]{2,1,0:T(8,128)(2,1)} %bitcast.15), calls=%async_computation | async-start | bytes 4194304 | tf_op jit(solution)/shard_map/all_to_all | solution.py:260
  15.0 0.1 add.80
  15.1 6.0 %fusion.3 = bf16[256,4096]{1,0:T(8,128)(2,1)} fusion(bf16[256,512]{1,0:T(8,128)(2,1)S(1)} %bitcast.16, f32[256]{0:T(256)S(1)} %add.80, f32[4096,512]{1,0:T(8,128)} %param.21), kind=kOutput, calls=%fused_computation.7 | convolution fusion | flops 1077936128 | bytes 10748928 | tf_op jit(solution)/shard_map/dot_general | solution.py:251
  21.1 41.5 %all-to-all-done.sky_ref = bf16[16,16,4096]{2,1,0:T(8,128)(2,1)S(1)} async-done(((bf16[16,16,4096]{2,1,0:T(8,128)(2,1)}), bf16[16,16,4096]{2,1,0:T(8,128)(2,1)S(1)}, u32[]{:S(2)}, u32[]{:S(2)}) %all-to-all-start) | async-done | bytes 2097184 | tf_op jit(solution)/shard_map/all_to_all | solution.py:260
  62.7 1.3 copy-done
  64.0 4.7 %all-to-all-start.2 = ((bf16[16,16,4096]{2,1,0:T(8,128)(2,1)}), bf16[16,16,4096]{2,1,0:T(8,128)(2,1)S(1)}, u32[]{:S(2)}, u32[]{:S(2)}) async-start(bf16[16,16,4096]{2,1,0:T(8,128)(2,1)} %bitcast.14), calls=%async_computation.2 | async-start | bytes 4194304 | tf_op jit(solution)/shard_map/all_to_all | solution.py:260
  68.7 0.0 copy-start.22
  68.7 3.9 %fusion.6 = (bf16[16,65536]{1,0:T(8,128)(2,1)}, bf16[16,65536]{1,0:T(8,128)(2,1)S(1)}) fusion(bf16[32,65536]{1,0:T(8,128)(2,1)} %param.23), kind=kLoop, calls=%fused_computation.23 | loop fusion | bytes 8388608 | tf_op jit(solution)/shard_map/slice | solution.py:261
  72.6 0.0 copy-start.9
  72.6 0.0 copy-start.10
  72.6 0.0 copy-start.11
  72.7 0.0 copy-start.13
  72.7 0.0 copy-start.15
  72.7 0.2 add_reduce_fusion
  72.9 0.1 select_reduce_fusion.order_ref
  73.0 0.1 broadcast_add_fusion
  73.1 0.0 copy-done.21
  73.1 0.7 copy_select_fusion
  73.8 0.1 pad_slice_fusion
  73.9 0.1 fusion.8
  74.0 0.2 copy-done.1
  74.2 0.1 copy-done.9
  74.3 0.1 copy-done.10
  74.4 0.1 copy-done.11
  74.4 0.0 copy-done.13
  74.5 0.0 copy-done.15
  74.5 44.6 %shard_map.228 = (bf16[16,65536]{1,0:T(8,128)(2,1)S(1)}, bf16[16,16,4096]{2,1,0:T(8,128)(2,1)S(1)}, f32[8,256]{1,0:T(8,128)S(1)}) custom-call(s32[4]{0:T(128)S(1)} %select_reduce_fusion.order_ref, f32[16]{0:T(128)S(1)} %get-tuple-element.25.noise_ref, bf16[16,16,4096]{2,1,0:T(8,128)(2,1)S(1)} %copy-done.1, bf16[16,65536]{1,0:T(8,128)(2,1)S(1)} %get-tuple-element.19.data_ref, ...), custom_call_target="tpu_custom_call" | custom-call | flops 11207180288 | bytes 8388608 | tf_op jit(solution)/shard_map/pallas_call | solution.py:188
  119.1 1.3 copy-done.2
  120.4 1.4 copy-done.4
  121.8 6.0 %all-to-all-start.1 = ((bf16[16,16,4096]{2,1,0:T(8,128)(2,1)}), bf16[16,16,4096]{2,1,0:T(8,128)(2,1)}, u32[]{:S(2)}, u32[]{:S(2)}) async-start(bf16[16,16,4096]{2,1,0:T(8,128)(2,1)} %copy-done.2), calls=%async_computation.1 | async-start | bytes 4194304 | tf_op jit(solution)/shard_map/all_to_all | solution.py:264
  127.8 0.6 reduce_sum.28
  128.4 1.6 copy-done.6
  130.0 0.9 copy-done.12
  130.9 0.9 copy-done.14
  131.9 0.9 copy-done.16
  132.8 44.6 %shard_map.229 = (bf16[16,65536]{1,0:T(8,128)(2,1)S(1)}, bf16[16,16,4096]{2,1,0:T(8,128)(2,1)S(1)}, f32[8,256]{1,0:T(8,128)S(1)}) custom-call(s32[4]{0:T(128)S(1)} %select_reduce_fusion.order_ref, f32[16]{0:T(128)S(1)} %get-tuple-element.24.noise_ref, bf16[16,16,4096]{2,1,0:T(8,128)(2,1)S(1)} %all-to-all-done.2.sky_ref, bf16[16,65536]{1,0:T(8,128)(2,1)S(1)} %copy-done.6, ...), custom_call_target="tpu_custom_call" | custom-call | flops 11207180288 | bytes 8388608 | tf_op jit(solution)/shard_map/pallas_call | solution.py:188
  177.4 1.3 copy-done.3
  178.7 1.3 copy-done.7
  180.0 0.6 reduce_sum.29
  181.9 6.0 %all-to-all-start.3 = ((bf16[16,16,4096]{2,1,0:T(8,128)(2,1)}), bf16[16,16,4096]{2,1,0:T(8,128)(2,1)}, u32[]{:S(2)}, u32[]{:S(2)}) async-start(bf16[16,16,4096]{2,1,0:T(8,128)(2,1)} %copy-done.3), calls=%async_computation.3 | async-start | bytes 4194304 | tf_op jit(solution)/shard_map/all_to_all | solution.py:264
  187.9 3.9 %pad_maximum_fusion = bf16[32,65536]{1,0:T(8,128)(2,1)} fusion(bf16[16,65536]{1,0:T(8,128)(2,1)} %copy-done.7, bf16[16,65536]{1,0:T(8,128)(2,1)S(1)} %copy-done.5), kind=kLoop, calls=%fused_computation.8 | loop fusion | flops 8388608 | bytes 8388608 | tf_op jit(solution)/shard_map/concatenate | solution.py:277
  191.8 62.3 %psum.7 = f32[]{:T(128)} all-reduce(f32[]{:T(128)S(6)} %add.86), channel_id=1, replica_groups=mesh['chain'=2,'pix'=16] {'pix'}, use_global_device_ids=true, to_apply=%region_3.4 | all-reduce | flops 1 | bytes 8 | tf_op jit(solution)/shard_map/psum | solution.py:266
  254.9 6.3 %fusion.9 = f32[4096,512]{1,0:T(8,128)} fusion(bf16[256,4096]{1,0:T(8,128)(2,1)} %bitcast.3, bf16[256,512]{1,0:T(8,128)(2,1)S(1)} %bitcast.19), kind=kOutput, calls=%fused_computation.26 | convolution fusion | flops 1073741824 | bytes 10747904 | tf_op jit(solution)/shard_map/dot_general | solution.py:269
  261.2 13.9 %multiply_add_fusion = (f32[4096,512]{1,0:T(8,128)}, f32[4096,512]{1,0:T(8,128)}) fusion(f32[4096,512]{1,0:T(8,128)} %param.21, f32[4096,512]{1,0:T(8,128)} %param.22, f32[4096,512]{1,0:T(8,128)} %fusion.9, bf16[256,4096]{1,0:T(8,128)(2,1)} %bitcast.6, bf16[256,512]{1,0:T(8,128)(2,1)S(1)} %bitcast.17), kind=kOutput, calls=%fused_computation | convolution fusion | flops 1086324736 | bytes 44302336 | tf_op jit(solution)/shard_map/dot_general | solution.py:269
  (34 shorter events, 0.1 us)
Async XLA Ops:
  2.6 6.2 %copy-start.19 = (bf16[16,1,16,512]{3,2,1,0:T(8,128)(2,1)}, bf16[16,1,16,512]{3,2,1,0:T(8,128)(2,1)S(1)}, u32[]{:S(2)}) copy-start(bf16[16,1,16,512]{3,2,1,0:T(8,128)(2,1)S(1)} %get-tuple-element.23) | copy-start | bytes 786436
  2.6 12.5 %copy-start.17 = (bf16[16,1,16,512]{3,2,1,0:T(8,128)(2,1)}, bf16[16,1,16,512]{3,2,1,0:T(8,128)(2,1)S(1)}, u32[]{:S(2)}) copy-start(bf16[16,1,16,512]{3,2,1,0:T(8,128)(2,1)S(1)} %get-tuple-element.22) | copy-start | bytes 786436
  8.8 53.8 %all-to-all-start = ((bf16[16,16,4096]{2,1,0:T(8,128)(2,1)}), bf16[16,16,4096]{2,1,0:T(8,128)(2,1)S(1)}, u32[]{:S(2)}, u32[]{:S(2)}) async-start(bf16[16,16,4096]{2,1,0:T(8,128)(2,1)} %bitcast.15), calls=%async_computation | async-start | bytes 4194304 | tf_op jit(solution)/shard_map/all_to_all | solution.py:260
  62.7 1.3 copy-start
  64.0 57.8 %all-to-all-start.2 = ((bf16[16,16,4096]{2,1,0:T(8,128)(2,1)}), bf16[16,16,4096]{2,1,0:T(8,128)(2,1)S(1)}, u32[]{:S(2)}, u32[]{:S(2)}) async-start(bf16[16,16,4096]{2,1,0:T(8,128)(2,1)} %bitcast.14), calls=%async_computation.2 | async-start | bytes 4194304 | tf_op jit(solution)/shard_map/all_to_all | solution.py:260
  68.7 3.9 %copy-start.24 = (s32[32]{0:T(128)S(1)}, s32[32]{0:T(128)}, u32[]{:S(2)}) copy-start(s32[32]{0:T(128)} %param.28) | copy-start | bytes 388
  68.7 4.0 %copy-start.22 = (s32[4,8]{1,0:T(4,128)S(1)}, s32[4,8]{1,0:T(4,128)}, u32[]{:S(2)}) copy-start(s32[4,8]{1,0:T(4,128)} %param.24) | copy-start | bytes 388
  68.7 4.4 %copy-start.21 = (f32[32,65,65]{2,0,1:T(8,128)S(1)}, f32[32,65,65]{2,0,1:T(8,128)}, u32[]{:S(2)}) copy-start(f32[32,65,65]{2,0,1:T(8,128)} %param.27) | copy-start | bytes 1622404
  72.6 1.3 copy-start.23
  72.6 1.6 copy-start.1
  72.6 1.6 copy-start.8
  72.6 1.7 copy-start.9
  72.6 1.7 copy-start.10
  72.6 1.8 copy-start.11
  72.7 1.8 copy-start.13
  72.7 1.8 copy-start.15
  119.1 1.3 copy-start.2
  120.4 1.4 copy-start.4
  121.8 60.1 %all-to-all-start.1 = ((bf16[16,16,4096]{2,1,0:T(8,128)(2,1)}), bf16[16,16,4096]{2,1,0:T(8,128)(2,1)}, u32[]{:S(2)}, u32[]{:S(2)}) async-start(bf16[16,16,4096]{2,1,0:T(8,128)(2,1)} %copy-done.2), calls=%async_computation.1 | async-start | bytes 4194304 | tf_op jit(solution)/shard_map/all_to_all | solution.py:264
  128.4 1.6 copy-start.6
  130.0 0.9 copy-start.12
  130.9 0.9 copy-start.14
  131.9 0.9 copy-start.16
  177.4 1.3 copy-start.3
  178.7 1.3 copy-start.7
  180.0 7.9 %copy-start.5 = (bf16[16,65536]{1,0:T(8,128)(2,1)S(1)}, bf16[16,65536]{1,0:T(8,128)(2,1)}, u32[]{:S(2)}) copy-start(bf16[16,65536]{1,0:T(8,128)(2,1)} %copy-done.4) | copy-start | bytes 6291460
  181.9 79.3 %all-to-all-start.3 = ((bf16[16,16,4096]{2,1,0:T(8,128)(2,1)}), bf16[16,16,4096]{2,1,0:T(8,128)(2,1)}, u32[]{:S(2)}, u32[]{:S(2)}) async-start(bf16[16,16,4096]{2,1,0:T(8,128)(2,1)} %copy-done.3), calls=%async_computation.3 | async-start | bytes 4194304 | tf_op jit(solution)/shard_map/all_to_all | solution.py:264
  187.9 66.9 %copy-start.20 = (bf16[16,1,16,512]{3,2,1,0:T(8,128)(2,1)S(1)}, bf16[16,1,16,512]{3,2,1,0:T(8,128)(2,1)}, u32[]{:S(2)}) copy-start(bf16[16,1,16,512]{3,2,1,0:T(8,128)(2,1)} %copy-done.19) | copy-start | bytes 786436
  254.9 6.3 %copy-start.18 = (bf16[16,1,16,512]{3,2,1,0:T(8,128)(2,1)S(1)}, bf16[16,1,16,512]{3,2,1,0:T(8,128)(2,1)}, u32[]{:S(2)}) copy-start(bf16[16,1,16,512]{3,2,1,0:T(8,128)(2,1)} %copy-done.17) | copy-start | bytes 786436

commit v2 on v1

v2 whole, which is shorter than its diff:
```python
import functools
import math

import jax
import jax.numpy as jnp
import numpy as np
from jax import lax
from jax.experimental import pallas as pl
from jax.experimental.pallas import tpu as pltpu
from jax.sharding import PartitionSpec as P

S = 128
R = 32
PATCHES = 4
TAPS = 65
SIDE = 2 * S
SPAN = SIDE + R
HALF = SPAN // 2
LANES = 256
TAP_ROWS = 80
TAP_LANES = 128
BLOCK = 16
VMEM_BYTES = 56 * 1024 * 1024
FLATTEN_VMEM_BYTES = 24 * 1024 * 1024
PIXEL_BLOCK = 1024
SKY_BLOCK = 2048

leap_size = 0.25


def half_tables(positions):
    angle = 2.0 * math.pi / SPAN * (np.arange(HALF)[:, None] + 0.5) * positions[None, :]
    return np.cos(angle), np.sin(angle)


def tables():
    low = jnp.bfloat16
    cos_image, sin_image = half_tables(np.arange(SIDE))
    cos_taps, sin_taps = half_tables(np.arange(TAPS) - R)
    rows = np.concatenate([cos_image, sin_image], axis=0)
    cols = np.zeros((2 * LANES, SIDE))
    cols[:HALF] = cos_image
    cols[LANES : LANES + HALF] = sin_image
    tap_rows = np.zeros((SPAN, TAP_ROWS))
    tap_rows[:, :TAPS] = np.concatenate([cos_taps, sin_taps], axis=0)
    tap_cols = np.zeros((TAP_LANES, 2 * LANES))
    tap_cols[:TAPS, :HALF] = cos_taps.T
    tap_cols[:TAPS, LANES : LANES + HALF] = sin_taps.T
    return (
        np.asarray(rows, low),
        np.asarray(rows.T, low),
        np.asarray(cols, low),
        np.asarray(cols.T, low),
        np.asarray(np.concatenate([tap_rows, tap_rows], axis=1), low),
        np.asarray(np.concatenate([tap_cols, tap_cols], axis=0), low),
    )


def dot(left, right):
    return lax.dot_general(
        left, right, (((1,), (0,)), ((), ())), preferred_element_type=jnp.float32
    )


def split_low(values):
    high = values.astype(jnp.bfloat16)
    return high, (values - high.astype(jnp.float32)).astype(jnp.bfloat16)


def strip_loop(order_ref, strip_rows, channels, body):
    strips = S // strip_rows

    def step(index, carry):
        cell = index // strips
        strip = index % strips
        device = order_ref[cell] * strips + strip
        base = (cell // 2) * S + strip * strip_rows
        pixel_base = device * (strip_rows * S)
        for row in range(strip_rows):
            body(
                cell % 2,
                device,
                pl.ds(row * S, S),
                pl.ds(base + row, channels, stride=SIDE),
                pl.ds(pl.multiple_of(pixel_base + row * S, S), S),
            )
        return carry

    lax.fori_loop(0, PATCHES * strips, step, 0)


def channel_rows(channel):
    return pl.ds(pl.multiple_of(channel * SIDE, SIDE), SIDE)


def signed_pair(values):
    cc, cs = values[:HALF, :LANES], values[:HALF, LANES:]
    sc, ss = values[HALF:, :LANES], values[HALF:, LANES:]
    return cc - ss, sc + cs, cc + ss, sc - cs


def prepare_kernel(
    strip_rows, order_ref, data_ref, taps_ref, tap_rows_ref, tap_cols_ref, beam_ref, image_ref, stack_ref
):
    channels = data_ref.shape[0]

    def spread(cell_col, device, lanes, spread_rows, pixels):
        stack_ref[cell_col, spread_rows, :] = data_ref[:, pixels].astype(jnp.float32)

    def channel_step(channel, carry):
        tap_high, tap_low = split_low(taps_ref[channel])
        tap_first = dot(tap_rows_ref[...], jnp.concatenate([tap_high, tap_low], axis=0))
        first_high, first_low = split_low(tap_first * (2.0 / (SPAN * SPAN)))
        spectrum = dot(jnp.concatenate([first_high, first_low], axis=1), tap_cols_ref[...])
        for part, values in enumerate(signed_pair(spectrum)):
            beam_ref[channel, part] = values
        here = channel_rows(channel)
        image_ref[channel, :, :S] = stack_ref[0, here, :].astype(jnp.bfloat16)
        image_ref[channel, :, S:] = stack_ref[1, here, :].astype(jnp.bfloat16)
        return carry

    strip_loop(order_ref, strip_rows, channels, spread)
    lax.fori_loop(0, channels, channel_step, 0)


def prepare(order, data, taps, strip_rows):
    channels, pixels = data.shape
    constants = tables()[4:]
    whole = pl.BlockSpec(memory_space=pltpu.VMEM)
    return pl.pallas_call(
        functools.partial(prepare_kernel, strip_rows),
        out_shape=(
            jax.ShapeDtypeStruct((channels, 4, HALF, LANES), jnp.float32),
            jax.ShapeDtypeStruct((channels, SIDE, SIDE), jnp.bfloat16),
        ),
        grid=(channels // BLOCK,),
        in_specs=[
            pl.BlockSpec(memory_space=pltpu.SMEM),
            pl.BlockSpec((BLOCK, pixels), lambda i: (i, 0)),
            pl.BlockSpec((BLOCK, TAP_ROWS, TAP_LANES), lambda i: (i, 0, 0)),
            whole,
            whole,
        ],
        out_specs=(
            pl.BlockSpec((BLOCK, 4, HALF, LANES), lambda i: (i, 0, 0, 0)),
            pl.BlockSpec((BLOCK, SIDE, SIDE), lambda i: (i, 0, 0)),
        ),
        scratch_shapes=[pltpu.VMEM((2, BLOCK * SIDE, S), jnp.float32)],
        compiler_params=pltpu.CompilerParams(vmem_limit_bytes=VMEM_BYTES),
        cost_estimate=pl.CostEstimate(
            flops=2 * channels * 1440 * 65536, bytes_accessed=28 << 20, transcendentals=0
        ),
    )(order, data, taps, *constants)


def convolve_kernel(
    strip_rows,
    first_channel,
    order_ref,
    noise_ref,
    earlier_ref,
    sky_ref,
    beam_ref,
    data_ref,
    rows_ref,
    rows_t_ref,
    cols_ref,
    cols_t_ref,
    residual_ref,
    grad_ref,
    misfit_ref,
    stack_ref,
):
    channel = pl.program_id(0)
    channels = sky_ref.shape[1]

    def spread(cell_col, device, lanes, spread_rows, pixels):
        stack_ref[cell_col, spread_rows, :] = sky_ref[device, :, lanes].astype(jnp.float32)

    def gather(cell_col, device, lanes, spread_rows, pixels):
        grad_ref[device, :, lanes] = stack_ref[cell_col, spread_rows, :].astype(jnp.bfloat16)

    def filter_image(image, conjugate):
        first = dot(rows_ref[...], image).astype(jnp.bfloat16)
        re_plus, im_plus, re_minus, im_minus = signed_pair(dot(first, cols_t_ref[...]))
        beam_re_plus, beam_im_plus, beam_re_minus, beam_im_minus = (
            beam_ref[0, 0],
            beam_ref[0, 1],
            beam_ref[0, 2],
            beam_ref[0, 3],
        )
        if conjugate:
            out_re_plus = re_plus * beam_re_plus + im_plus * beam_im_plus
            out_im_plus = im_plus * beam_re_plus - re_plus * beam_im_plus
            out_re_minus = re_minus * beam_re_minus + im_minus * beam_im_minus
            out_im_minus = im_minus * beam_re_minus - re_minus * beam_im_minus
        else:
            out_re_plus = re_plus * beam_re_plus - im_plus * beam_im_plus
            out_im_plus = im_plus * beam_re_plus + re_plus * beam_im_plus
            out_re_minus = re_minus * beam_re_minus - im_minus * beam_im_minus
            out_im_minus = im_minus * beam_re_minus + re_minus * beam_im_minus
        product = jnp.concatenate(
            [
                jnp.concatenate([out_re_plus + out_re_minus, out_im_plus - out_im_minus], axis=1),
                jnp.concatenate([out_im_plus + out_im_minus, out_re_minus - out_re_plus], axis=1),
            ],
            axis=0,
        ).astype(jnp.bfloat16)
        second = dot(product, cols_ref[...]).astype(jnp.bfloat16)
        return dot(rows_t_ref[...], second)

    @pl.when(channel == 0)
    def _():
        misfit_ref[...] = earlier_ref[...]
        strip_loop(order_ref, strip_rows, channels, spread)

    here = channel_rows(channel)
    image = jnp.concatenate([stack_ref[0, here, :], stack_ref[1, here, :]], axis=1)
    residual = filter_image(image.astype(jnp.bfloat16), True) - data_ref[0].astype(jnp.float32)
    residual_ref[0] = residual.astype(jnp.bfloat16)
    weighted = noise_ref[first_channel + channel] * residual
    misfit_ref[...] += jnp.sum((weighted * residual).reshape(SIDE // 8, 8, SIDE), axis=0)
    grad = filter_image(weighted.astype(jnp.bfloat16), False) * image
    stack_ref[0, here, :] = grad[:, :S]
    stack_ref[1, here, :] = grad[:, S:]

    @pl.when(channel == channels - 1)
    def _():
        strip_loop(order_ref, strip_rows, channels, gather)
        strip = strip_rows * S
        if grad_ref.shape[2] > strip:
            total = jnp.full((channels, S), jnp.sum(misfit_ref[...]), jnp.float32)
            high, rest = split_low(total)
            middle = rest.astype(jnp.float32)
            low = total - high.astype(jnp.float32) - middle
            lane = lax.broadcasted_iota(jnp.int32, (channels, S), 1)
            terms = jnp.where(lane == 0, high.astype(jnp.float32), jnp.where(lane == 1, middle, low))
            terms = jnp.where(lane < 3, terms, 0.0).astype(jnp.bfloat16)
            for device in range(grad_ref.shape[0]):
                grad_ref[device, :, strip:] = terms


def convolve(order, noise_weight, earlier, sky, beam, data_images, chunk, extra):
    devices, channels, strip = sky.shape
    smem = pl.BlockSpec(memory_space=pltpu.SMEM)
    whole = pl.BlockSpec(memory_space=pltpu.VMEM)
    constants = tables()[:4]
    first_channel = chunk * channels
    return pl.pallas_call(
        functools.partial(convolve_kernel, strip // S, first_channel),
        out_shape=(
            jax.ShapeDtypeStruct((channels, SIDE, SIDE), jnp.bfloat16),
            jax.ShapeDtypeStruct((devices, channels, strip + extra), jnp.bfloat16),
            jax.ShapeDtypeStruct((8, SIDE), jnp.float32),
        ),
        grid=(channels,),
        in_specs=[
            smem,
            smem,
            whole,
            whole,
            pl.BlockSpec((1, 4, HALF, LANES), lambda i: (first_channel + i, 0, 0, 0)),
            pl.BlockSpec((1, SIDE, SIDE), lambda i: (first_channel + i, 0, 0)),
        ]
        + [whole] * len(constants),
        out_specs=(pl.BlockSpec((1, SIDE, SIDE), lambda i: (i, 0, 0)), whole, whole),
        scratch_shapes=[pltpu.VMEM((2, channels * SIDE, S), jnp.float32)],
        compiler_params=pltpu.CompilerParams(vmem_limit_bytes=VMEM_BYTES),
        cost_estimate=pl.CostEstimate(
            flops=2 * channels * 2 * 1952 * 65536, bytes_accessed=24 << 20, transcendentals=0
        ),
    )(order, noise_weight, earlier, sky, beam, data_images, *constants)


def flatten_kernel(strip_rows, order_ref, *refs):
    image_refs, flat_ref, stack_ref = refs[:-2], refs[-2], refs[-1]
    for chunk, image_ref in enumerate(image_refs):
        channels = image_ref.shape[0]
        rows = slice(chunk * channels, (chunk + 1) * channels)

        def channel_step(channel, carry):
            here = channel_rows(channel)
            image = image_ref[channel].astype(jnp.float32)
            stack_ref[0, here, :] = image[:, :S]
            stack_ref[1, here, :] = image[:, S:]
            return carry

        def gather(cell_col, device, lanes, spread_rows, pixels):
            flat_ref[rows, pixels] = stack_ref[cell_col, spread_rows, :].astype(jnp.bfloat16)

        lax.fori_loop(0, channels, channel_step, 0)
        strip_loop(order_ref, strip_rows, channels, gather)


def flatten(order, images, strip_rows):
    channels = sum(part.shape[0] for part in images)
    whole = pl.BlockSpec(memory_space=pltpu.VMEM)
    return pl.pallas_call(
        functools.partial(flatten_kernel, strip_rows),
        out_shape=jax.ShapeDtypeStruct((channels, SIDE * SIDE), jnp.bfloat16),
        in_specs=[pl.BlockSpec(memory_space=pltpu.SMEM)] + [whole] * len(images),
        out_specs=whole,
        scratch_shapes=[pltpu.VMEM((2, images[0].shape[0] * SIDE, S), jnp.float32)],
        compiler_params=pltpu.CompilerParams(vmem_limit_bytes=FLATTEN_VMEM_BYTES),
        cost_estimate=pl.CostEstimate(flops=1 << 20, bytes_accessed=32 << 20, transcendentals=0),
    )(order, *images)


def sky_kernel(chunk, root_ref, level_ref, latent_ref, sky_ref):
    devices, _, channels, freqs = root_ref.shape
    pixels = latent_ref.shape[0]
    root = root_ref[:, 0].reshape(devices * channels, freqs)
    log_sky = lax.dot_general(
        root,
        latent_ref[...].astype(jnp.bfloat16),
        (((1,), (1,)), ((), ())),
        preferred_element_type=jnp.float32,
    )
    level = jnp.broadcast_to(level_ref[...], (S, freqs)).T.reshape(devices, -1, channels, S)
    level = level[:, chunk].reshape(devices * channels, S)
    for first in range(0, pixels, S):
        sky = jnp.exp(log_sky[:, first : first + S] + level).astype(jnp.bfloat16)
        sky_ref[:, :, first : first + S] = sky.reshape(devices, channels, S)


def brightness(chunk, root_parts, log_level, latent):
    devices, _, channels, freqs = root_parts.shape
    pixels = latent.shape[0]
    return pl.pallas_call(
        functools.partial(sky_kernel, chunk),
        out_shape=jax.ShapeDtypeStruct((devices, channels, pixels), jnp.bfloat16),
        grid=(pixels // SKY_BLOCK,),
        in_specs=[
            pl.BlockSpec((devices, 1, channels, freqs), lambda i: (0, chunk, 0, 0)),
            pl.BlockSpec((1, freqs), lambda i: (0, 0)),
            pl.BlockSpec((SKY_BLOCK, freqs), lambda i: (i, 0)),
        ],
        out_specs=pl.BlockSpec((devices, channels, SKY_BLOCK), lambda i: (0, 0, i)),
        compiler_params=pltpu.CompilerParams(vmem_limit_bytes=VMEM_BYTES),
        cost_estimate=pl.CostEstimate(
            flops=2 * pixels * freqs * devices * channels,
            bytes_accessed=10 << 20,
            transcendentals=pixels * devices * channels,
        ),
    )(root_parts, log_level.reshape(1, freqs), latent)


def pull_back(chunk, grad_ref, root_ref, here):
    devices, channels, _ = grad_ref.shape
    return lax.dot_general(
        grad_ref[:, :, here].reshape(devices * channels, here.size),
        root_ref[:, chunk].reshape(devices * channels, -1),
        (((0,), (0,)), ((), ())),
        preferred_element_type=jnp.float32,
    )


def kick_kernel(grad_count, momentum_ref, latent_ref, root_ref, *refs):
    far_refs, kicked_ref, grad_refs = refs[:grad_count], refs[grad_count], refs[grad_count + 1 :]
    pixels = latent_ref.shape[0]
    here = pl.ds(pl.multiple_of(pl.program_id(0) * pixels, pixels), pixels)

    @pl.when(pl.program_id(0) == 0)
    def _():
        for far_ref, grad_ref in zip(far_refs, grad_refs):
            pltpu.sync_copy(far_ref, grad_ref)

    force = latent_ref[...]
    for chunk, grad_ref in enumerate(grad_refs):
        force = force + pull_back(chunk, grad_ref, root_ref, here)
    kicked_ref[...] = momentum_ref[...] - leap_size * force


def kick(momentum, latent, root_parts, grads):
    pixels, freqs = latent.shape
    block = pl.BlockSpec((PIXEL_BLOCK, freqs), lambda i: (i, 0))
    far = pl.BlockSpec(memory_space=pltpu.HBM)
    return pl.pallas_call(
        functools.partial(kick_kernel, len(grads)),
        out_shape=jax.ShapeDtypeStruct(latent.shape, jnp.float32),
        grid=(pixels // PIXEL_BLOCK,),
        in_specs=[block, block, pl.BlockSpec(memory_space=pltpu.VMEM)] + [far] * len(grads),
        out_specs=block,
        scratch_shapes=[pltpu.VMEM(grad.shape, grad.dtype) for grad in grads],
        compiler_params=pltpu.CompilerParams(vmem_limit_bytes=VMEM_BYTES),
        cost_estimate=pl.CostEstimate(
            flops=2 * pixels * freqs * 256, bytes_accessed=26 << 20, transcendentals=0
        ),
    )(momentum, latent, root_parts, *grads)


def leap_kernel(
    chunk,
    scale,
    kicked_ref,
    latent_ref,
    grad_ref,
    root_ref,
    latent_out_ref,
    momentum_out_ref,
    misfit_ref,
):
    pixels = momentum_out_ref.shape[0]
    here = pl.ds(pl.multiple_of(pl.program_id(0) * pixels, pixels), pixels)
    grad_latent = pull_back(chunk, grad_ref, root_ref, here)
    momentum = kicked_ref[...] - leap_size * grad_latent
    momentum_out_ref[...] = momentum
    latent_out_ref[...] = latent_ref[...] + leap_size * momentum

    @pl.when(pl.program_id(0) == 0)
    def _():
        terms = grad_ref[:, :, grad_ref.shape[2] - S :].astype(jnp.float32)
        row = lax.broadcasted_iota(jnp.int32, terms.shape, 1)
        misfit_ref[0] = scale * jnp.sum(jnp.where(row == 0, terms, 0.0))


def leap(chunk, scale, kicked, latent, grad, root_parts):
    pixels, freqs = latent.shape
    whole = pl.BlockSpec(memory_space=pltpu.VMEM)
    block = pl.BlockSpec((PIXEL_BLOCK, freqs), lambda i: (i, 0))
    return pl.pallas_call(
        functools.partial(leap_kernel, chunk, scale),
        out_shape=(jax.ShapeDtypeStruct(latent.shape, jnp.float32),) * 2
        + (jax.ShapeDtypeStruct((1,), jnp.float32),),
        grid=(pixels // PIXEL_BLOCK,),
        in_specs=[block, block, whole, whole],
        out_specs=(block, block, pl.BlockSpec(memory_space=pltpu.SMEM)),
        compiler_params=pltpu.CompilerParams(vmem_limit_bytes=VMEM_BYTES),
        cost_estimate=pl.CostEstimate(
            flops=2 * pixels * freqs * 256, bytes_accessed=34 << 20, transcendentals=0
        ),
    )(kicked, latent, grad, root_parts)


def cell_order(neighbours):
    has_above = neighbours[:, 1] != -1
    has_left = neighbours[:, 3] != -1
    cells = 2 * has_above.astype(jnp.int32) + has_left.astype(jnp.int32)
    patch_ids = jnp.arange(PATCHES, dtype=jnp.int32)
    match = cells[None, :] == patch_ids[:, None]
    return jnp.sum(jnp.where(match, patch_ids[None, :], 0), axis=1)


def masked_taps(beam_taps, beam_radius):
    offsets = jnp.arange(TAPS, dtype=jnp.int32) - R
    distance = offsets[:, None] * offsets[:, None] + offsets[None, :] * offsets[None, :]
    inside = distance[None, :, :] <= (beam_radius * beam_radius)[:, None, None]
    kernel = jnp.where(inside, beam_taps, jnp.zeros_like(beam_taps))
    return jnp.pad(kernel, ((0, 0), (0, TAP_ROWS - TAPS), (0, TAP_LANES - TAPS)))


def shards(
    latent,
    momentum,
    data,
    neighbours,
    spectral_root,
    log_level,
    beam_taps,
    beam_radius,
    noise_weight,
):
    devices = lax.axis_size("pix")
    pix_dev = latent.shape[0]
    chan_dev = data.shape[0]
    freqs = spectral_root.shape[0]
    chunks = chan_dev // BLOCK
    root_parts = spectral_root.reshape(devices, chunks, BLOCK, freqs)
    order = cell_order(neighbours)
    taps = masked_taps(beam_taps, beam_radius)

    strip_rows = pix_dev // S
    beam, data_images = prepare(order, data, taps, strip_rows)

    skies = []
    for chunk in range(chunks):
        level = log_level
        if chunk == 1:
            level, beam, data_images = lax.optimization_barrier((level, beam, data_images))
        skies.append(brightness(chunk, root_parts, level, latent))

    residuals, grads = [], []
    partial = jnp.zeros((8, SIDE), jnp.float32)
    for chunk in range(chunks):
        extra = S if chunk == chunks - 1 else 0
        sky = lax.all_to_all(skies[chunk], "pix", split_axis=0, concat_axis=0, tiled=True)
        residual, grad, partial = convolve(
            order, noise_weight, partial, sky, beam, data_images, chunk, extra
        )
        residuals.append(residual)
        grads.append(lax.all_to_all(grad, "pix", split_axis=0, concat_axis=0, tiled=True))

    residual_maps = flatten(order, residuals, strip_rows)
    kicked = kick(momentum, latent, root_parts, grads[:-1])
    scale = 0.5 / (freqs * devices * pix_dev)
    new_latent, new_momentum, misfit = leap(
        chunks - 1, scale, kicked, latent, grads[-1], root_parts
    )
    return (new_latent, new_momentum, residual_maps, misfit)


def solution(mesh):
    placed = (
        P(("chain", "pix"), None),
        P(("chain", "pix"), None),
        P("pix", "chain"),
        P("chain", None),
        P(),
        P(),
        P("pix", None, None),
        P("pix"),
        P("pix"),
    )
    return jax.shard_map(
        shards,
        mesh=mesh,
        in_specs=placed,
        out_specs=(
            P(("chain", "pix"), None),
            P(("chain", "pix"), None),
            P("pix", "chain"),
            P("chain"),
        ),
        check_vma=False,
    )
```

time: 277 us -> 233 us (0.84)
  blocking collectives: 62.3 us -> 0 us
  Pallas kernels: 89.2 us -> 149 us
  matrix products: 32.4 us -> 0 us
  waiting for transfers between devices: 41.6 us -> 56.7 us
  local copies, waits for them, and re-layouts: 17.6 us -> 4.67 us
  other arithmetic: 6.19 us -> 1.6 us
  between operations: 3.91 us -> 0.71 us
    psum x1 -> x0, blocking collectives: 62.3 us -> none  [shards(): lax.psum(sum(partials), 'pix')]
    pallas_call x2 -> x8, Pallas kernels: 89.2 us -> 149 us  [the longest x2 77.9 us: convolve(): pl.pallas_call(functools.partial(convolve_kernel, strip // S, first_chann...]
    all_to_all x2, waiting for transfers between devices: 0.01 us -> 35.5 us  [shards(): lax.all_to_all(grad, 'pix', split_axis=0, concat_axis=0, tiled=True)]
    dot_general x4 -> x0, matrix products: 32.4 us -> none  [the longest x2 20.2 us: shards(): lax.dot_general(grads[chunk].reshape(devices * BLOCK, pix_dev), root_part...]
    all_to_all x2, waiting for transfers between devices: 41.6 us -> 21.1 us  [shards(): lax.all_to_all(skies[chunk], 'pix', split_axis=0, concat_axis=0, tiled=True)]
    unnamed x50 -> x16, local copies, waits for them, and re-layouts: 11.5 us -> 2.94 us
    slice x5 -> x0, local copies, waits for them, and re-layouts: 5.18 us -> none  [the longest x1 3.9 us: shards(): data[here]]
    concatenate x1 -> x0, other arithmetic: 3.92 us -> none  [shards(): residual_maps = jnp.concatenate(residuals, axis=0)]
  transfers between devices with their start and end apart: 4 -> 4, of which waited for: 1 -> 4; matrix products, arithmetic and copies ran while one was open for 8% -> 1% of each run, Pallas kernels for 32% -> 56%
where the time goes in v2:
time: 233 us
  Pallas kernels  149 us (64%)
  waiting for transfers between devices  56.7 us (24%)
  starting transfers between devices  20.5 us (9%)
  local copies, waits for them, and re-layouts  4.67 us (2%)
    pallas_call x2, Pallas kernels, convolve(): pl.pallas_call(functools.partial(convolve_kernel, strip // S, first_chann...  77.9 us
    all_to_all x2, waiting for transfers between devices, shards(): lax.all_to_all(grad, 'pix', split_axis=0, concat_axis=0, tiled=True)  35.5 us
    pallas_call x1, Pallas kernels, prepare(): pl.pallas_call(functools.partial(prepare_kernel, strip_rows), out_shape=(...  26.6 us
    all_to_all x2, waiting for transfers between devices, shards(): lax.all_to_all(skies[chunk], 'pix', split_axis=0, concat_axis=0, tiled=True)  21.1 us
    pallas_call x1, Pallas kernels, leap(): pl.pallas_call(functools.partial(leap_kernel, chunk, scale), out_shape=(j...  12.7 us
    pallas_call x1, Pallas kernels, kick(): pl.pallas_call(functools.partial(kick_kernel, len(grads)), out_shape=jax....  11.7 us
    all_to_all x2, starting transfers between devices, shards(): lax.all_to_all(skies[chunk], 'pix', split_axis=0, concat_axis=0, tiled=True)  11 us
    pallas_call x2, Pallas kernels, brightness(): pl.pallas_call(functools.partial(sky_kernel, chunk), out_shape=jax.ShapeD...  10.8 us
  transfers between devices with their start and end apart: 4, of which 4 were waited for; matrix products, arithmetic and copies ran while one was open for 1% of the time, Pallas kernels for 56%

profile of v2, /device:TPU:16, one launch (start us, length us, event | category | flops | bytes accessed | tf_op | source)
XLA Modules:
  0.0 232.7 jit_solution(8261690740468322947)
XLA Ops:
  0.6 5.3 %shard_map.210 = bf16[16,16,4096]{2,1,0:T(8,128)(2,1)} custom-call(bf16[16,2,16,512]{3,2,1,0:T(8,128)(2,1)} %bitcast.3, f32[1,512]{1,0:T(1,128)} %bitcast.7, f32[4096,512]{1,0:T(8,128)} %latent_ref.7), custom_call_target="tpu_custom_call" | custom-call | flops 1073741824 | bytes 10485760 | tf_op jit(solution)/shard_map/pallas_call | solution.py:329
  6.0 0.0 copy-start.7
  6.0 0.0 copy-start.5
  6.0 6.3 %all-to-all-start = ((bf16[16,16,4096]{2,1,0:T(8,128)(2,1)}), bf16[16,16,4096]{2,1,0:T(8,128)(2,1)S(1)}, u32[]{:S(2)}, u32[]{:S(2)}) async-start(bf16[16,16,4096]{2,1,0:T(8,128)(2,1)} %shard_map.210), calls=%async_computation | async-start | bytes 4194304 | tf_op jit(solution)/shard_map/all_to_all | solution.py:486
  12.3 0.0 copy-done.7
  12.3 0.1 broadcast_add_fusion
  12.4 0.0 copy-done.5
  12.4 0.0 copy-start.6
  12.4 0.7 copy_select_fusion
  13.1 1.1 pad.4.taps_ref
  14.3 0.0 copy-done.6
  14.3 0.2 add_reduce_fusion
  14.4 0.6 select_reduce_fusion.order_ref
  15.1 26.6 %shard_map.211 = (f32[32,4,144,256]{3,2,1,0:T(8,128)}, bf16[32,256,256]{2,1,0:T(8,128)(2,1)}) custom-call(s32[4]{0:T(128)} %select_reduce_fusion.order_ref, bf16[32,65536]{1,0:T(8,128)(2,1)} %data_ref.1, f32[32,80,128]{2,1,0:T(8,128)} %pad.4.taps_ref, bf16[288,160]{1,0:T(8,128)(2,1)} %constant.26.clone.tap_rows_ref, bf16[256,512]{1,0:T(8,128)(2,1)} %constant.27.clone.tap_cols_ref), custom_call_target="tpu_custom_call" | custom-call | flops 6039797760 | bytes 29360128 | tf_op jit(solution)/shard_map/pallas_call | solution.py:130
  41.7 5.5 %shard_map.214 = bf16[16,16,4096]{2,1,0:T(8,128)(2,1)} custom-call(bf16[16,2,16,512]{3,2,1,0:T(8,128)(2,1)} %bitcast.4, f32[1,512]{1,0:T(1,128)} %bitcast.8, f32[4096,512]{1,0:T(8,128)} %latent_ref.7), custom_call_target="tpu_custom_call" | custom-call | flops 1073741824 | bytes 10485760 | tf_op jit(solution)/shard_map/pallas_call | solution.py:329
  47.1 12.8 %all-to-all-done.sky_ref = bf16[16,16,4096]{2,1,0:T(8,128)(2,1)S(1)} async-done(((bf16[16,16,4096]{2,1,0:T(8,128)(2,1)}), bf16[16,16,4096]{2,1,0:T(8,128)(2,1)S(1)}, u32[]{:S(2)}, u32[]{:S(2)}) %all-to-all-start) | async-done | bytes 2097184 | tf_op jit(solution)/shard_map/all_to_all | solution.py:486
  59.9 0.0 copy-start.4
  59.9 4.7 %all-to-all-start.2 = ((bf16[16,16,4096]{2,1,0:T(8,128)(2,1)}), bf16[16,16,4096]{2,1,0:T(8,128)(2,1)}, u32[]{:S(2)}, u32[]{:S(2)}) async-start(bf16[16,16,4096]{2,1,0:T(8,128)(2,1)} %shard_map.214), calls=%async_computation.2 | async-start | bytes 4194304 | tf_op jit(solution)/shard_map/all_to_all | solution.py:486
  64.6 0.6 broadcast_in_dim.18.earlier_ref
  65.2 0.0 copy-done.4
  65.2 38.8 %shard_map.212 = (bf16[16,256,256]{2,1,0:T(8,128)(2,1)}, bf16[16,16,4096]{2,1,0:T(8,128)(2,1)}, f32[8,256]{1,0:T(8,128)}) custom-call(s32[4]{0:T(128)} %select_reduce_fusion.order_ref, f32[32]{0:T(128)} %noise_ref.3, f32[8,256]{1,0:T(8,128)} %broadcast_in_dim.18.earlier_ref, bf16[16,16,4096]{2,1,0:T(8,128)(2,1)} %copy-done.4, ...), custom_call_target="tpu_custom_call" | custom-call | flops 8187281408 | bytes 25165824 | tf_op jit(solution)/shard_map/pallas_call | solution.py:249
  104.0 8.3 %all-to-all-done.2.sky_ref = bf16[16,16,4096]{2,1,0:T(8,128)(2,1)} async-done(((bf16[16,16,4096]{2,1,0:T(8,128)(2,1)}), bf16[16,16,4096]{2,1,0:T(8,128)(2,1)}, u32[]{:S(2)}, u32[]{:S(2)}) %all-to-all-start.2) | async-done | bytes 2097184 | tf_op jit(solution)/shard_map/all_to_all | solution.py:486
  112.4 4.7 %all-to-all-start.1 = ((bf16[16,16,4096]{2,1,0:T(8,128)(2,1)}), bf16[16,16,4096]{2,1,0:T(8,128)(2,1)S(1)}, u32[]{:S(2)}, u32[]{:S(2)}) async-start(bf16[16,16,4096]{2,1,0:T(8,128)(2,1)} %get-tuple-element.21), calls=%async_computation.1 | async-start | bytes 4194304 | tf_op jit(solution)/shard_map/all_to_all | solution.py:491
  117.0 39.1 %shard_map.215 = (bf16[16,256,256]{2,1,0:T(8,128)(2,1)}, bf16[16,16,4224]{2,1,0:T(8,128)(2,1)}, f32[8,256]{1,0:T(8,128)}) custom-call(s32[4]{0:T(128)} %select_reduce_fusion.order_ref, f32[32]{0:T(128)} %noise_ref.3, f32[8,256]{1,0:T(8,128)} %get-tuple-element.22.earlier_ref, bf16[16,16,4096]{2,1,0:T(8,128)(2,1)} %all-to-all-done.2.sky_ref, ...), custom_call_target="tpu_custom_call" | custom-call | flops 8187281408 | bytes 25165824 | tf_op jit(solution)/shard_map/pallas_call | solution.py:249
  156.1 8.6 %all-to-all-done.1.refs_0_ = bf16[16,16,4096]{2,1,0:T(8,128)(2,1)S(1)} async-done(((bf16[16,16,4096]{2,1,0:T(8,128)(2,1)}), bf16[16,16,4096]{2,1,0:T(8,128)(2,1)S(1)}, u32[]{:S(2)}, u32[]{:S(2)}) %all-to-all-start.1) | async-done | bytes 2097184 | tf_op jit(solution)/shard_map/all_to_all | solution.py:491
  164.7 0.0 copy-start.3
  164.7 1.3 copy-done.3
  166.0 0.0 copy-start
  166.0 0.0 copy-start.2
  166.0 4.8 %all-to-all-start.3 = ((bf16[16,16,4224]{2,1,0:T(8,128)(2,1)}), bf16[16,16,4224]{2,1,0:T(8,128)(2,1)}, u32[]{:S(2)}, u32[]{:S(2)}) async-start(bf16[16,16,4224]{2,1,0:T(8,128)(2,1)} %get-tuple-element.24), calls=%async_computation.3 | async-start | bytes 4325376 | tf_op jit(solution)/shard_map/all_to_all | solution.py:491
  170.8 0.0 copy-done
  170.8 0.0 copy-done.2
  170.9 0.0 copy-start.1
  170.9 1.6 copy-done.1
  172.4 8.9 %shard_map.217 = bf16[32,65536]{1,0:T(8,128)(2,1)} custom-call(s32[4]{0:T(128)S(1)} %copy-done.2, bf16[16,256,256]{2,1,0:T(8,128)(2,1)S(1)} %copy-done, bf16[16,256,256]{2,1,0:T(8,128)(2,1)S(1)} %copy-done.1), custom_call_target="tpu_custom_call" | custom-call | flops 1048576 | bytes 33554432 | tf_op jit(solution)/shard_map/pallas_call | solution.py:298
  181.3 11.7 %shard_map.213.kicked_ref = f32[4096,512]{1,0:T(8,128)} custom-call(f32[4096,512]{1,0:T(8,128)} %momentum_ref.1, f32[4096,512]{1,0:T(8,128)} %latent_ref.7, bf16[16,2,16,512]{3,2,1,0:T(8,128)(2,1)} %bitcast.5, bf16[16,16,4096]{2,1,0:T(8,128)(2,1)} %copy-done.3), custom_call_target="tpu_custom_call" | custom-call | flops 1073741824 | bytes 27262976 | tf_op jit(solution)/shard_map/pallas_call | solution.py:378
  193.0 27.0 %all-to-all-done.3.grad_ref = bf16[16,16,4224]{2,1,0:T(8,128)(2,1)} async-done(((bf16[16,16,4224]{2,1,0:T(8,128)(2,1)}), bf16[16,16,4224]{2,1,0:T(8,128)(2,1)}, u32[]{:S(2)}, u32[]{:S(2)}) %all-to-all-start.3) | async-done | bytes 2162720 | tf_op jit(solution)/shard_map/all_to_all | solution.py:491
  220.0 12.7 %shard_map.216 = (f32[4096,512]{1,0:T(8,128)}, f32[4096,512]{1,0:T(8,128)}, f32[1]{0:T(128)}) custom-call(f32[4096,512]{1,0:T(8,128)} %shard_map.213.kicked_ref, f32[4096,512]{1,0:T(8,128)} %latent_ref.7, bf16[16,16,4224]{2,1,0:T(8,128)(2,1)} %all-to-all-done.3.grad_ref, bf16[16,2,16,512]{3,2,1,0:T(8,128)(2,1)} %bitcast.6), custom_call_target="tpu_custom_call" | custom-call | flops 1073741824 | bytes 35651584 | tf_op jit(solution)/shard_map/pallas_call | solution.py:421
  (2 shorter events, 0.0 us)
Async XLA Ops:
  6.0 6.3 %copy-start.7 = (s32[32]{0:T(128)S(1)}, s32[32]{0:T(128)}, u32[]{:S(2)}) copy-start(s32[32]{0:T(128)} %param.26) | copy-start | bytes 388
  6.0 6.4 %copy-start.5 = (f32[32,65,65]{2,0,1:T(8,128)S(1)}, f32[32,65,65]{2,0,1:T(8,128)}, u32[]{:S(2)}) copy-start(f32[32,65,65]{2,0,1:T(8,128)} %param.25) | copy-start | bytes 1622404
  6.0 54.0 %all-to-all-start = ((bf16[16,16,4096]{2,1,0:T(8,128)(2,1)}), bf16[16,16,4096]{2,1,0:T(8,128)(2,1)S(1)}, u32[]{:S(2)}, u32[]{:S(2)}) async-start(bf16[16,16,4096]{2,1,0:T(8,128)(2,1)} %shard_map.210), calls=%async_computation | async-start | bytes 4194304 | tf_op jit(solution)/shard_map/all_to_all | solution.py:486
  12.4 1.9 copy-start.6
  59.9 5.3 %copy-start.4 = (bf16[16,16,4096]{2,1,0:T(8,128)(2,1)}, bf16[16,16,4096]{2,1,0:T(8,128)(2,1)S(1)}, u32[]{:S(2)}) copy-start(bf16[16,16,4096]{2,1,0:T(8,128)(2,1)S(1)} %all-to-all-done.sky_ref) | copy-start | bytes 6291460
  59.9 52.4 %all-to-all-start.2 = ((bf16[16,16,4096]{2,1,0:T(8,128)(2,1)}), bf16[16,16,4096]{2,1,0:T(8,128)(2,1)}, u32[]{:S(2)}, u32[]{:S(2)}) async-start(bf16[16,16,4096]{2,1,0:T(8,128)(2,1)} %shard_map.214), calls=%async_computation.2 | async-start | bytes 4194304 | tf_op jit(solution)/shard_map/all_to_all | solution.py:486
  112.4 52.3 %all-to-all-start.1 = ((bf16[16,16,4096]{2,1,0:T(8,128)(2,1)}), bf16[16,16,4096]{2,1,0:T(8,128)(2,1)S(1)}, u32[]{:S(2)}, u32[]{:S(2)}) async-start(bf16[16,16,4096]{2,1,0:T(8,128)(2,1)} %get-tuple-element.21), calls=%async_computation.1 | async-start | bytes 4194304 | tf_op jit(solution)/shard_map/all_to_all | solution.py:491
  164.7 1.3 copy-start.3
  166.0 4.8 %copy-start = (bf16[16,256,256]{2,1,0:T(8,128)(2,1)S(1)}, bf16[16,256,256]{2,1,0:T(8,128)(2,1)}, u32[]{:S(2)}) copy-start(bf16[16,256,256]{2,1,0:T(8,128)(2,1)} %get-tuple-element.27.refs_0_) | copy-start | bytes 6291460
  166.0 4.8 %copy-start.2 = (s32[4]{0:T(128)S(1)}, s32[4]{0:T(128)}, u32[]{:S(2)}) copy-start(s32[4]{0:T(128)} %select_reduce_fusion.order_ref) | copy-start | bytes 52
  166.0 54.0 %all-to-all-start.3 = ((bf16[16,16,4224]{2,1,0:T(8,128)(2,1)}), bf16[16,16,4224]{2,1,0:T(8,128)(2,1)}, u32[]{:S(2)}, u32[]{:S(2)}) async-start(bf16[16,16,4224]{2,1,0:T(8,128)(2,1)} %get-tuple-element.24), calls=%async_computation.3 | async-start | bytes 4325376 | tf_op jit(solution)/shard_map/all_to_all | solution.py:491
  170.9 1.6 copy-start.1

commit v3 on v2

--- a/solution.py
+++ b/solution.py
@@ -355,15 +355,10 @@
     )
 
 
-def kick_kernel(grad_count, momentum_ref, latent_ref, root_ref, *refs):
-    far_refs, kicked_ref, grad_refs = refs[:grad_count], refs[grad_count], refs[grad_count + 1 :]
+def kick_kernel(momentum_ref, latent_ref, root_ref, *refs):
+    grad_refs, kicked_ref = refs[:-1], refs[-1]
     pixels = latent_ref.shape[0]
     here = pl.ds(pl.multiple_of(pl.program_id(0) * pixels, pixels), pixels)
-
-    @pl.when(pl.program_id(0) == 0)
-    def _():
-        for far_ref, grad_ref in zip(far_refs, grad_refs):
-            pltpu.sync_copy(far_ref, grad_ref)
 
     force = latent_ref[...]
     for chunk, grad_ref in enumerate(grad_refs):
@@ -374,15 +369,14 @@
 def kick(momentum, latent, root_parts, grads):
     pixels, freqs = latent.shape
     block = pl.BlockSpec((PIXEL_BLOCK, freqs), lambda i: (i, 0))
-    far = pl.BlockSpec(memory_space=pltpu.HBM)
+    whole = pl.BlockSpec(memory_space=pltpu.VMEM)
     return pl.pallas_call(
-        functools.partial(kick_kernel, len(grads)),
+        kick_kernel,
         out_shape=jax.ShapeDtypeStruct(latent.shape, jnp.float32),
         grid=(pixels // PIXEL_BLOCK,),
-        in_specs=[block, block, pl.BlockSpec(memory_space=pltpu.VMEM)] + [far] * len(grads),
+        in_specs=[block, block] + [whole] * (1 + len(grads)),
         out_specs=block,
-        scratch_shapes=[pltpu.VMEM(grad.shape, grad.dtype) for grad in grads],
-        compiler_params=pltpu.CompilerParams(vmem_limit_bytes=VMEM_BYTES),
+        compiler_params=pltpu.CompilerParams(vmem_limit_bytes=FLATTEN_VMEM_BYTES),
         cost_estimate=pl.CostEstimate(
             flops=2 * pixels * freqs * 256, bytes_accessed=26 << 20, transcendentals=0
         ),
@@ -395,21 +389,21 @@
     kicked_ref,
     latent_ref,
     grad_ref,
+    terms_ref,
     root_ref,
     latent_out_ref,
     momentum_out_ref,
     misfit_ref,
 ):
     pixels = momentum_out_ref.shape[0]
-    here = pl.ds(pl.multiple_of(pl.program_id(0) * pixels, pixels), pixels)
-    grad_latent = pull_back(chunk, grad_ref, root_ref, here)
+    grad_latent = pull_back(chunk, grad_ref, root_ref, pl.ds(0, pixels))
     momentum = kicked_ref[...] - leap_size * grad_latent
     momentum_out_ref[...] = momentum
     latent_out_ref[...] = latent_ref[...] + leap_size * momentum
 
     @pl.when(pl.program_id(0) == 0)
     def _():
-        terms = grad_ref[:, :, grad_ref.shape[2] - S :].astype(jnp.float32)
+        terms = terms_ref[...].astype(jnp.float32)
         row = lax.broadcasted_iota(jnp.int32, terms.shape, 1)
         misfit_ref[0] = scale * jnp.sum(jnp.where(row == 0, terms, 0.0))
 
@@ -417,19 +411,20 @@
 def leap(chunk, scale, kicked, latent, grad, root_parts):
     pixels, freqs = latent.shape
     whole = pl.BlockSpec(memory_space=pltpu.VMEM)
+    far_grad = pltpu.with_memory_space_constraint(grad, pltpu.HBM)
     block = pl.BlockSpec((PIXEL_BLOCK, freqs), lambda i: (i, 0))
     return pl.pallas_call(
         functools.partial(leap_kernel, chunk, scale),
         out_shape=(jax.ShapeDtypeStruct(latent.shape, jnp.float32),) * 2
         + (jax.ShapeDtypeStruct((1,), jnp.float32),),
         grid=(pixels // PIXEL_BLOCK,),
-        in_specs=[block, block, whole, whole],
+        in_specs=[block, block, pl.BlockSpec(grad.shape[:2] + (PIXEL_BLOCK,), lambda i: (0, 0, i)), pl.BlockSpec(grad.shape[:2] + (S,), lambda i: (0, 0, pixels // S)), whole],
         out_specs=(block, block, pl.BlockSpec(memory_space=pltpu.SMEM)),
         compiler_params=pltpu.CompilerParams(vmem_limit_bytes=VMEM_BYTES),
         cost_estimate=pl.CostEstimate(
             flops=2 * pixels * freqs * 256, bytes_accessed=34 << 20, transcendentals=0
         ),
-    )(kicked, latent, grad, root_parts)
+    )(kicked, latent, far_grad, far_grad, root_parts)
 
 
 def cell_order(neighbours):

time: 233 us -> 233 us (level)
  local copies, waits for them, and re-layouts: 4.67 us -> 16.3 us
  Pallas kernels: 149 us -> 138 us
    unnamed x16 -> x22, local copies, waits for them, and re-layouts: 2.94 us -> 14.5 us
    pallas_call x1, Pallas kernels: 11.7 us -> 1.93 us  [kick(): pl.pallas_call(kick_kernel, out_shape=jax.ShapeDtypeStruct(latent.shape,...]
  transfers between devices with their start and end apart: 4 -> 4, of which waited for: 4 -> 4; matrix products, arithmetic and copies ran while one was open for 1% -> 1% of each run, Pallas kernels for 56% -> 52%
where the time goes in v3:
time: 233 us; the launch traced here: 232 us
  Pallas kernels  138 us (59%)
  waiting for transfers between devices  55 us (24%)
  starting transfers between devices  20.5 us (9%)
  local copies, waits for them, and re-layouts  16.3 us (7%)
    pallas_call x2, Pallas kernels, convolve(): pl.pallas_call(functools.partial(convolve_kernel, strip // S, first_chann...  77.9 us
    all_to_all x2, waiting for transfers between devices, shards(): lax.all_to_all(grad, 'pix', split_axis=0, concat_axis=0, tiled=True)  33.7 us
    pallas_call x1, Pallas kernels, prepare(): pl.pallas_call(functools.partial(prepare_kernel, strip_rows), out_shape=(...  26.6 us
    all_to_all x2, waiting for transfers between devices, shards(): lax.all_to_all(skies[chunk], 'pix', split_axis=0, concat_axis=0, tiled=True)  21.2 us
    unnamed x22, local copies, waits for them, and re-layouts  14.5 us
    pallas_call x1, Pallas kernels, leap(): pl.pallas_call(functools.partial(leap_kernel, chunk, scale), out_shape=(j...  12.3 us
    all_to_all x2, starting transfers between devices, shards(): lax.all_to_all(skies[chunk], 'pix', split_axis=0, concat_axis=0, tiled=True)  11 us
    pallas_call x2, Pallas kernels, brightness(): pl.pallas_call(functools.partial(sky_kernel, chunk), out_shape=jax.ShapeD...  10.7 us
  transfers between devices with their start and end apart: 4, of which 4 were waited for; matrix products, arithmetic and copies ran while one was open for 1% of the time, Pallas kernels for 52%

profile of v3, /device:TPU:16, one launch (start us, length us, event | category | flops | bytes accessed | tf_op | source)
XLA Modules:
  0.0 232.3 jit_solution(12998046995369558016)
XLA Ops:
  0.6 5.3 %shard_map.210 = bf16[16,16,4096]{2,1,0:T(8,128)(2,1)} custom-call(bf16[16,2,16,512]{3,2,1,0:T(8,128)(2,1)} %bitcast.3, f32[1,512]{1,0:T(1,128)} %bitcast.7, f32[4096,512]{1,0:T(8,128)} %latent_ref.7), custom_call_target="tpu_custom_call" | custom-call | flops 1073741824 | bytes 10485760 | tf_op jit(solution)/shard_map/pallas_call | solution.py:329
  6.0 0.0 copy-start.10
  6.0 0.0 copy-start.8
  6.0 6.3 %all-to-all-start = ((bf16[16,16,4096]{2,1,0:T(8,128)(2,1)}), bf16[16,16,4096]{2,1,0:T(8,128)(2,1)}, u32[]{:S(2)}, u32[]{:S(2)}) async-start(bf16[16,16,4096]{2,1,0:T(8,128)(2,1)} %shard_map.210), calls=%async_computation | async-start | bytes 4194304 | tf_op jit(solution)/shard_map/all_to_all | solution.py:481
  12.3 0.0 copy-done.10
  12.3 0.1 broadcast_add_fusion
  12.4 0.0 copy-done.8
  12.4 0.0 copy-start.9
  12.4 0.7 copy_select_fusion
  13.1 1.1 pad.4.taps_ref
  14.3 0.0 copy-done.9
  14.3 0.2 add_reduce_fusion
  14.4 0.6 select_reduce_fusion.order_ref
  15.1 26.6 %shard_map.211 = (f32[32,4,144,256]{3,2,1,0:T(8,128)}, bf16[32,256,256]{2,1,0:T(8,128)(2,1)}) custom-call(s32[4]{0:T(128)} %select_reduce_fusion.order_ref, bf16[32,65536]{1,0:T(8,128)(2,1)} %data_ref.1, f32[32,80,128]{2,1,0:T(8,128)} %pad.4.taps_ref, bf16[288,160]{1,0:T(8,128)(2,1)} %constant.26.clone.tap_rows_ref, bf16[256,512]{1,0:T(8,128)(2,1)} %constant.27.clone.tap_cols_ref), custom_call_target="tpu_custom_call" | custom-call | flops 6039797760 | bytes 29360128 | tf_op jit(solution)/shard_map/pallas_call | solution.py:130
  41.7 5.4 %shard_map.214 = bf16[16,16,4096]{2,1,0:T(8,128)(2,1)} custom-call(bf16[16,2,16,512]{3,2,1,0:T(8,128)(2,1)} %bitcast.4, f32[1,512]{1,0:T(1,128)} %bitcast.8, f32[4096,512]{1,0:T(8,128)} %latent_ref.7), custom_call_target="tpu_custom_call" | custom-call | flops 1073741824 | bytes 10485760 | tf_op jit(solution)/shard_map/pallas_call | solution.py:329
  47.1 13.0 %all-to-all-done.sky_ref = bf16[16,16,4096]{2,1,0:T(8,128)(2,1)} async-done(((bf16[16,16,4096]{2,1,0:T(8,128)(2,1)}), bf16[16,16,4096]{2,1,0:T(8,128)(2,1)}, u32[]{:S(2)}, u32[]{:S(2)}) %all-to-all-start) | async-done | bytes 2097184 | tf_op jit(solution)/shard_map/all_to_all | solution.py:481
  60.0 4.7 %all-to-all-start.2 = ((bf16[16,16,4096]{2,1,0:T(8,128)(2,1)}), bf16[16,16,4096]{2,1,0:T(8,128)(2,1)S(1)}, u32[]{:S(2)}, u32[]{:S(2)}) async-start(bf16[16,16,4096]{2,1,0:T(8,128)(2,1)} %shard_map.214), calls=%async_computation.2 | async-start | bytes 4194304 | tf_op jit(solution)/shard_map/all_to_all | solution.py:481
  64.7 0.6 broadcast_in_dim.18.earlier_ref
  65.3 38.8 %shard_map.212 = (bf16[16,256,256]{2,1,0:T(8,128)(2,1)}, bf16[16,16,4096]{2,1,0:T(8,128)(2,1)}, f32[8,256]{1,0:T(8,128)}) custom-call(s32[4]{0:T(128)} %select_reduce_fusion.order_ref, f32[32]{0:T(128)} %noise_ref.3, f32[8,256]{1,0:T(8,128)} %broadcast_in_dim.18.earlier_ref, bf16[16,16,4096]{2,1,0:T(8,128)(2,1)} %all-to-all-done.sky_ref, ...), custom_call_target="tpu_custom_call" | custom-call | flops 8187281408 | bytes 25165824 | tf_op jit(solution)/shard_map/pallas_call | solution.py:249
  104.1 8.3 %all-to-all-done.2.sky_ref = bf16[16,16,4096]{2,1,0:T(8,128)(2,1)S(1)} async-done(((bf16[16,16,4096]{2,1,0:T(8,128)(2,1)}), bf16[16,16,4096]{2,1,0:T(8,128)(2,1)S(1)}, u32[]{:S(2)}, u32[]{:S(2)}) %all-to-all-start.2) | async-done | bytes 2097184 | tf_op jit(solution)/shard_map/all_to_all | solution.py:481
  112.4 0.0 copy-start.7
  112.4 1.3 copy-done.7
  113.7 4.7 %all-to-all-start.1 = ((bf16[16,16,4096]{2,1,0:T(8,128)(2,1)}), bf16[16,16,4096]{2,1,0:T(8,128)(2,1)S(1)}, u32[]{:S(2)}, u32[]{:S(2)}) async-start(bf16[16,16,4096]{2,1,0:T(8,128)(2,1)} %get-tuple-element.21), calls=%async_computation.1 | async-start | bytes 4194304 | tf_op jit(solution)/shard_map/all_to_all | solution.py:486
  118.4 39.1 %shard_map.215 = (bf16[16,256,256]{2,1,0:T(8,128)(2,1)}, bf16[16,16,4224]{2,1,0:T(8,128)(2,1)}, f32[8,256]{1,0:T(8,128)}) custom-call(s32[4]{0:T(128)} %select_reduce_fusion.order_ref, f32[32]{0:T(128)} %noise_ref.3, f32[8,256]{1,0:T(8,128)} %get-tuple-element.22.earlier_ref, bf16[16,16,4096]{2,1,0:T(8,128)(2,1)} %copy-done.7, ...), custom_call_target="tpu_custom_call" | custom-call | flops 8187281408 | bytes 25165824 | tf_op jit(solution)/shard_map/pallas_call | solution.py:249
  157.5 8.6 %all-to-all-done.1.refs_0_ = bf16[16,16,4096]{2,1,0:T(8,128)(2,1)S(1)} async-done(((bf16[16,16,4096]{2,1,0:T(8,128)(2,1)}), bf16[16,16,4096]{2,1,0:T(8,128)(2,1)S(1)}, u32[]{:S(2)}, u32[]{:S(2)}) %all-to-all-start.1) | async-done | bytes 2097184 | tf_op jit(solution)/shard_map/all_to_all | solution.py:486
  166.0 0.0 copy-start.6
  166.0 4.8 %all-to-all-start.3 = ((bf16[16,16,4224]{2,1,0:T(8,128)(2,1)}), bf16[16,16,4224]{2,1,0:T(8,128)(2,1)}, u32[]{:S(2)}, u32[]{:S(2)}) async-start(bf16[16,16,4224]{2,1,0:T(8,128)(2,1)} %get-tuple-element.24), calls=%async_computation.3 | async-start | bytes 4325376 | tf_op jit(solution)/shard_map/all_to_all | solution.py:486
  170.9 0.0 copy-done.6
  170.9 0.0 copy-start.4
  170.9 1.6 copy-done.4
  172.5 0.0 copy-start.5
  172.5 1.6 copy-done.5
  174.1 0.0 copy-start.3
  174.1 8.9 %shard_map.217 = bf16[32,65536]{1,0:T(8,128)(2,1)} custom-call(s32[4]{0:T(128)S(1)} %copy-done.6, bf16[16,256,256]{2,1,0:T(8,128)(2,1)S(1)} %copy-done.4, bf16[16,256,256]{2,1,0:T(8,128)(2,1)S(1)} %copy-done.5), custom_call_target="tpu_custom_call" | custom-call | flops 1048576 | bytes 33554432 | tf_op jit(solution)/shard_map/pallas_call | solution.py:298
  182.9 0.0 copy-done.3
  182.9 0.0 copy-start
  182.9 3.4 %copy-done = f32[4096,512]{1,0:T(8,128)S(1)} copy-done((f32[4096,512]{1,0:T(8,128)S(1)}, f32[4096,512]{1,0:T(8,128)}, u32[]{:S(2)}) %copy-start) | copy-done | bytes 8388632
  186.3 0.0 copy-start.2
  186.3 3.4 %copy-done.2 = f32[4096,512]{1,0:T(8,128)S(1)} copy-done((f32[4096,512]{1,0:T(8,128)S(1)}, f32[4096,512]{1,0:T(8,128)}, u32[]{:S(2)}) %copy-start.2) | copy-done | bytes 8388632
  189.7 1.9 shard_map.213.kicked_ref
  191.6 0.0 copy-start.1
  191.6 3.2 %copy-done.1 = f32[4096,512]{1,0:T(8,128)} copy-done((f32[4096,512]{1,0:T(8,128)}, f32[4096,512]{1,0:T(8,128)S(1)}, u32[]{:S(2)}) %copy-start.1) | copy-done | bytes 8388632
  194.9 25.2 %all-to-all-done.3.grad_ref.terms_ref = bf16[16,16,4224]{2,1,0:T(8,128)(2,1)} async-done(((bf16[16,16,4224]{2,1,0:T(8,128)(2,1)}), bf16[16,16,4224]{2,1,0:T(8,128)(2,1)}, u32[]{:S(2)}, u32[]{:S(2)}) %all-to-all-start.3) | async-done | bytes 2162720 | tf_op jit(solution)/shard_map/all_to_all | solution.py:486
  220.0 12.3 %shard_map.216 = (f32[4096,512]{1,0:T(8,128)}, f32[4096,512]{1,0:T(8,128)}, f32[1]{0:T(128)}) custom-call(f32[4096,512]{1,0:T(8,128)} %copy-done.1, f32[4096,512]{1,0:T(8,128)} %latent_ref.7, bf16[16,16,4224]{2,1,0:T(8,128)(2,1)} %all-to-all-done.3.grad_ref.terms_ref, bf16[16,16,4224]{2,1,0:T(8,128)(2,1)} %all-to-all-done.3.grad_ref.terms_ref, ...), custom_call_target="tpu_custom_call" | custom-call | flops 1073741824 | bytes 35651584 | tf_op jit(solution)/shard_map/pallas_call | solution.py:416
  (2 shorter events, 0.0 us)
Async XLA Ops:
  6.0 6.3 %copy-start.10 = (s32[32]{0:T(128)S(1)}, s32[32]{0:T(128)}, u32[]{:S(2)}) copy-start(s32[32]{0:T(128)} %param.26) | copy-start | bytes 388
  6.0 6.4 %copy-start.8 = (f32[32,65,65]{2,0,1:T(8,128)S(1)}, f32[32,65,65]{2,0,1:T(8,128)}, u32[]{:S(2)}) copy-start(f32[32,65,65]{2,0,1:T(8,128)} %param.25) | copy-start | bytes 1622404
  6.0 54.1 %all-to-all-start = ((bf16[16,16,4096]{2,1,0:T(8,128)(2,1)}), bf16[16,16,4096]{2,1,0:T(8,128)(2,1)}, u32[]{:S(2)}, u32[]{:S(2)}) async-start(bf16[16,16,4096]{2,1,0:T(8,128)(2,1)} %shard_map.210), calls=%async_computation | async-start | bytes 4194304 | tf_op jit(solution)/shard_map/all_to_all | solution.py:481
  12.4 1.9 copy-start.9
  60.0 52.3 %all-to-all-start.2 = ((bf16[16,16,4096]{2,1,0:T(8,128)(2,1)}), bf16[16,16,4096]{2,1,0:T(8,128)(2,1)S(1)}, u32[]{:S(2)}, u32[]{:S(2)}) async-start(bf16[16,16,4096]{2,1,0:T(8,128)(2,1)} %shard_map.214), calls=%async_computation.2 | async-start | bytes 4194304 | tf_op jit(solution)/shard_map/all_to_all | solution.py:481
  112.4 1.4 copy-start.7
  113.7 52.3 %all-to-all-start.1 = ((bf16[16,16,4096]{2,1,0:T(8,128)(2,1)}), bf16[16,16,4096]{2,1,0:T(8,128)(2,1)S(1)}, u32[]{:S(2)}, u32[]{:S(2)}) async-start(bf16[16,16,4096]{2,1,0:T(8,128)(2,1)} %get-tuple-element.21), calls=%async_computation.1 | async-start | bytes 4194304 | tf_op jit(solution)/shard_map/all_to_all | solution.py:486
  166.0 4.8 %copy-start.6 = (s32[4]{0:T(128)S(1)}, s32[4]{0:T(128)}, u32[]{:S(2)}) copy-start(s32[4]{0:T(128)} %select_reduce_fusion.order_ref) | copy-start | bytes 52
  166.0 54.0 %all-to-all-start.3 = ((bf16[16,16,4224]{2,1,0:T(8,128)(2,1)}), bf16[16,16,4224]{2,1,0:T(8,128)(2,1)}, u32[]{:S(2)}, u32[]{:S(2)}) async-start(bf16[16,16,4224]{2,1,0:T(8,128)(2,1)} %get-tuple-element.24), calls=%async_computation.3 | async-start | bytes 4325376 | tf_op jit(solution)/shard_map/all_to_all | solution.py:486
  170.9 1.6 copy-start.4
  172.5 1.6 copy-start.5
  174.1 8.9 %copy-start.3 = (bf16[512,512]{1,0:T(8,128)(2,1)S(1)}, bf16[512,512]{1,0:T(8,128)(2,1)}, u32[]{:S(2)}) copy-start(bf16[512,512]{1,0:T(8,128)(2,1)} %param.23) | copy-start | bytes 1572868
  182.9 3.4 %copy-start = (f32[4096,512]{1,0:T(8,128)S(1)}, f32[4096,512]{1,0:T(8,128)}, u32[]{:S(2)}) copy-start(f32[4096,512]{1,0:T(8,128)} %latent_ref.7) | copy-start | bytes 25165828
  186.3 3.4 %copy-start.2 = (f32[4096,512]{1,0:T(8,128)S(1)}, f32[4096,512]{1,0:T(8,128)}, u32[]{:S(2)}) copy-start(f32[4096,512]{1,0:T(8,128)} %momentum_ref.1) | copy-start | bytes 25165828
  191.6 3.2 %copy-start.1 = (f32[4096,512]{1,0:T(8,128)}, f32[4096,512]{1,0:T(8,128)S(1)}, u32[]{:S(2)}) copy-start(f32[4096,512]{1,0:T(8,128)S(1)} %shard_map.213.kicked_ref) | copy-start | bytes 25165828

commit v4 on v3

--- a/solution.py
+++ b/solution.py
@@ -23,6 +23,7 @@
 VMEM_BYTES = 56 * 1024 * 1024
 FLATTEN_VMEM_BYTES = 24 * 1024 * 1024
 PIXEL_BLOCK = 1024
+LEAP_BLOCK = 2048
 SKY_BLOCK = 2048
 
 leap_size = 0.25
@@ -412,13 +413,13 @@
     pixels, freqs = latent.shape
     whole = pl.BlockSpec(memory_space=pltpu.VMEM)
     far_grad = pltpu.with_memory_space_constraint(grad, pltpu.HBM)
-    block = pl.BlockSpec((PIXEL_BLOCK, freqs), lambda i: (i, 0))
+    block = pl.BlockSpec((LEAP_BLOCK, freqs), lambda i: (i, 0))
     return pl.pallas_call(
         functools.partial(leap_kernel, chunk, scale),
         out_shape=(jax.ShapeDtypeStruct(latent.shape, jnp.float32),) * 2
         + (jax.ShapeDtypeStruct((1,), jnp.float32),),
-        grid=(pixels // PIXEL_BLOCK,),
-        in_specs=[block, block, pl.BlockSpec(grad.shape[:2] + (PIXEL_BLOCK,), lambda i: (0, 0, i)), pl.BlockSpec(grad.shape[:2] + (S,), lambda i: (0, 0, pixels // S)), whole],
+        grid=(pixels // LEAP_BLOCK,),
+        in_specs=[block, block, pl.BlockSpec(grad.shape[:2] + (LEAP_BLOCK,), lambda i: (0, 0, i)), pl.BlockSpec(grad.shape[:2] + (S,), lambda i: (0, 0, pixels // S)), whole],
         out_specs=(block, block, pl.BlockSpec(memory_space=pltpu.SMEM)),
         compiler_params=pltpu.CompilerParams(vmem_limit_bytes=VMEM_BYTES),
         cost_estimate=pl.CostEstimate(

time: 233 us -> 233 us (level)
  no operation moved by 1% of the time
where the time goes in v4:
time: 233 us
  Pallas kernels  138 us (59%)
  waiting for transfers between devices  55 us (24%)
  starting transfers between devices  20.5 us (9%)
  local copies, waits for them, and re-layouts  16.3 us (7%)
    pallas_call x2, Pallas kernels, convolve(): pl.pallas_call(functools.partial(convolve_kernel, strip // S, first_chann...  77.9 us
    all_to_all x2, waiting for transfers between devices, shards(): lax.all_to_all(grad, 'pix', split_axis=0, concat_axis=0, tiled=True)  33.7 us
    pallas_call x1, Pallas kernels, prepare(): pl.pallas_call(functools.partial(prepare_kernel, strip_rows), out_shape=(...  26.6 us
    all_to_all x2, waiting for transfers between devices, shards(): lax.all_to_all(skies[chunk], 'pix', split_axis=0, concat_axis=0, tiled=True)  21.2 us
    unnamed x22, local copies, waits for them, and re-layouts  14.5 us
    pallas_call x1, Pallas kernels, leap(): pl.pallas_call(functools.partial(leap_kernel, chunk, scale), out_shape=(j...  12.5 us
    all_to_all x2, starting transfers between devices, shards(): lax.all_to_all(skies[chunk], 'pix', split_axis=0, concat_axis=0, tiled=True)  11 us
    pallas_call x2, Pallas kernels, brightness(): pl.pallas_call(functools.partial(sky_kernel, chunk), out_shape=jax.ShapeD...  10.7 us
  transfers between devices with their start and end apart: 4, of which 4 were waited for; matrix products, arithmetic and copies ran while one was open for 1% of the time, Pallas kernels for 52%

profile of v4, /device:TPU:16, one launch (start us, length us, event | category | flops | bytes accessed | tf_op | source)
XLA Modules:
  0.0 232.5 jit_solution(14764469374527081492)
XLA Ops:
  0.6 5.3 %shard_map.210 = bf16[16,16,4096]{2,1,0:T(8,128)(2,1)} custom-call(bf16[16,2,16,512]{3,2,1,0:T(8,128)(2,1)} %bitcast.3, f32[1,512]{1,0:T(1,128)} %bitcast.7, f32[4096,512]{1,0:T(8,128)} %latent_ref.7), custom_call_target="tpu_custom_call" | custom-call | flops 1073741824 | bytes 10485760 | tf_op jit(solution)/shard_map/pallas_call | solution.py:330
  6.0 0.0 copy-start.10
  6.0 0.0 copy-start.8
  6.0 6.3 %all-to-all-start = ((bf16[16,16,4096]{2,1,0:T(8,128)(2,1)}), bf16[16,16,4096]{2,1,0:T(8,128)(2,1)}, u32[]{:S(2)}, u32[]{:S(2)}) async-start(bf16[16,16,4096]{2,1,0:T(8,128)(2,1)} %shard_map.210), calls=%async_computation | async-start | bytes 4194304 | tf_op jit(solution)/shard_map/all_to_all | solution.py:482
  12.3 0.0 copy-done.10
  12.3 0.1 broadcast_add_fusion
  12.4 0.0 copy-done.8
  12.4 0.0 copy-start.9
  12.4 0.7 copy_select_fusion
  13.1 1.1 pad.4.taps_ref
  14.3 0.0 copy-done.9
  14.3 0.2 add_reduce_fusion
  14.4 0.6 select_reduce_fusion.order_ref
  15.1 26.6 %shard_map.211 = (f32[32,4,144,256]{3,2,1,0:T(8,128)}, bf16[32,256,256]{2,1,0:T(8,128)(2,1)}) custom-call(s32[4]{0:T(128)} %select_reduce_fusion.order_ref, bf16[32,65536]{1,0:T(8,128)(2,1)} %data_ref.1, f32[32,80,128]{2,1,0:T(8,128)} %pad.4.taps_ref, bf16[288,160]{1,0:T(8,128)(2,1)} %constant.26.clone.tap_rows_ref, bf16[256,512]{1,0:T(8,128)(2,1)} %constant.27.clone.tap_cols_ref), custom_call_target="tpu_custom_call" | custom-call | flops 6039797760 | bytes 29360128 | tf_op jit(solution)/shard_map/pallas_call | solution.py:131
  41.7 5.4 %shard_map.214 = bf16[16,16,4096]{2,1,0:T(8,128)(2,1)} custom-call(bf16[16,2,16,512]{3,2,1,0:T(8,128)(2,1)} %bitcast.4, f32[1,512]{1,0:T(1,128)} %bitcast.8, f32[4096,512]{1,0:T(8,128)} %latent_ref.7), custom_call_target="tpu_custom_call" | custom-call | flops 1073741824 | bytes 10485760 | tf_op jit(solution)/shard_map/pallas_call | solution.py:330
  47.1 13.0 %all-to-all-done.sky_ref = bf16[16,16,4096]{2,1,0:T(8,128)(2,1)} async-done(((bf16[16,16,4096]{2,1,0:T(8,128)(2,1)}), bf16[16,16,4096]{2,1,0:T(8,128)(2,1)}, u32[]{:S(2)}, u32[]{:S(2)}) %all-to-all-start) | async-done | bytes 2097184 | tf_op jit(solution)/shard_map/all_to_all | solution.py:482
  60.0 4.7 %all-to-all-start.2 = ((bf16[16,16,4096]{2,1,0:T(8,128)(2,1)}), bf16[16,16,4096]{2,1,0:T(8,128)(2,1)S(1)}, u32[]{:S(2)}, u32[]{:S(2)}) async-start(bf16[16,16,4096]{2,1,0:T(8,128)(2,1)} %shard_map.214), calls=%async_computation.2 | async-start | bytes 4194304 | tf_op jit(solution)/shard_map/all_to_all | solution.py:482
  64.7 0.6 broadcast_in_dim.18.earlier_ref
  65.3 38.8 %shard_map.212 = (bf16[16,256,256]{2,1,0:T(8,128)(2,1)}, bf16[16,16,4096]{2,1,0:T(8,128)(2,1)}, f32[8,256]{1,0:T(8,128)}) custom-call(s32[4]{0:T(128)} %select_reduce_fusion.order_ref, f32[32]{0:T(128)} %noise_ref.3, f32[8,256]{1,0:T(8,128)} %broadcast_in_dim.18.earlier_ref, bf16[16,16,4096]{2,1,0:T(8,128)(2,1)} %all-to-all-done.sky_ref, ...), custom_call_target="tpu_custom_call" | custom-call | flops 8187281408 | bytes 25165824 | tf_op jit(solution)/shard_map/pallas_call | solution.py:250
  104.1 8.3 %all-to-all-done.2.sky_ref = bf16[16,16,4096]{2,1,0:T(8,128)(2,1)S(1)} async-done(((bf16[16,16,4096]{2,1,0:T(8,128)(2,1)}), bf16[16,16,4096]{2,1,0:T(8,128)(2,1)S(1)}, u32[]{:S(2)}, u32[]{:S(2)}) %all-to-all-start.2) | async-done | bytes 2097184 | tf_op jit(solution)/shard_map/all_to_all | solution.py:482
  112.4 0.0 copy-start.7
  112.4 1.3 copy-done.7
  113.7 4.7 %all-to-all-start.1 = ((bf16[16,16,4096]{2,1,0:T(8,128)(2,1)}), bf16[16,16,4096]{2,1,0:T(8,128)(2,1)S(1)}, u32[]{:S(2)}, u32[]{:S(2)}) async-start(bf16[16,16,4096]{2,1,0:T(8,128)(2,1)} %get-tuple-element.21), calls=%async_computation.1 | async-start | bytes 4194304 | tf_op jit(solution)/shard_map/all_to_all | solution.py:487
  118.4 39.1 %shard_map.215 = (bf16[16,256,256]{2,1,0:T(8,128)(2,1)}, bf16[16,16,4224]{2,1,0:T(8,128)(2,1)}, f32[8,256]{1,0:T(8,128)}) custom-call(s32[4]{0:T(128)} %select_reduce_fusion.order_ref, f32[32]{0:T(128)} %noise_ref.3, f32[8,256]{1,0:T(8,128)} %get-tuple-element.22.earlier_ref, bf16[16,16,4096]{2,1,0:T(8,128)(2,1)} %copy-done.7, ...), custom_call_target="tpu_custom_call" | custom-call | flops 8187281408 | bytes 25165824 | tf_op jit(solution)/shard_map/pallas_call | solution.py:250
  157.5 8.6 %all-to-all-done.1.refs_0_ = bf16[16,16,4096]{2,1,0:T(8,128)(2,1)S(1)} async-done(((bf16[16,16,4096]{2,1,0:T(8,128)(2,1)}), bf16[16,16,4096]{2,1,0:T(8,128)(2,1)S(1)}, u32[]{:S(2)}, u32[]{:S(2)}) %all-to-all-start.1) | async-done | bytes 2097184 | tf_op jit(solution)/shard_map/all_to_all | solution.py:487
  166.0 0.0 copy-start.6
  166.0 4.8 %all-to-all-start.3 = ((bf16[16,16,4224]{2,1,0:T(8,128)(2,1)}), bf16[16,16,4224]{2,1,0:T(8,128)(2,1)}, u32[]{:S(2)}, u32[]{:S(2)}) async-start(bf16[16,16,4224]{2,1,0:T(8,128)(2,1)} %get-tuple-element.24), calls=%async_computation.3 | async-start | bytes 4325376 | tf_op jit(solution)/shard_map/all_to_all | solution.py:487
  170.9 0.0 copy-done.6
  170.9 0.0 copy-start.4
  170.9 1.6 copy-done.4
  172.5 0.0 copy-start.5
  172.5 1.6 copy-done.5
  174.1 0.0 copy-start.3
  174.1 8.9 %shard_map.217 = bf16[32,65536]{1,0:T(8,128)(2,1)} custom-call(s32[4]{0:T(128)S(1)} %copy-done.6, bf16[16,256,256]{2,1,0:T(8,128)(2,1)S(1)} %copy-done.4, bf16[16,256,256]{2,1,0:T(8,128)(2,1)S(1)} %copy-done.5), custom_call_target="tpu_custom_call" | custom-call | flops 1048576 | bytes 33554432 | tf_op jit(solution)/shard_map/pallas_call | solution.py:299
  182.9 0.0 copy-done.3
  182.9 0.0 copy-start
  182.9 3.4 %copy-done = f32[4096,512]{1,0:T(8,128)S(1)} copy-done((f32[4096,512]{1,0:T(8,128)S(1)}, f32[4096,512]{1,0:T(8,128)}, u32[]{:S(2)}) %copy-start) | copy-done | bytes 8388632
  186.3 0.0 copy-start.2
  186.3 3.4 %copy-done.2 = f32[4096,512]{1,0:T(8,128)S(1)} copy-done((f32[4096,512]{1,0:T(8,128)S(1)}, f32[4096,512]{1,0:T(8,128)}, u32[]{:S(2)}) %copy-start.2) | copy-done | bytes 8388632
  189.7 1.9 shard_map.213.kicked_ref
  191.6 0.0 copy-start.1
  191.6 3.2 %copy-done.1 = f32[4096,512]{1,0:T(8,128)} copy-done((f32[4096,512]{1,0:T(8,128)}, f32[4096,512]{1,0:T(8,128)S(1)}, u32[]{:S(2)}) %copy-start.1) | copy-done | bytes 8388632
  194.9 25.2 %all-to-all-done.3.grad_ref.terms_ref = bf16[16,16,4224]{2,1,0:T(8,128)(2,1)} async-done(((bf16[16,16,4224]{2,1,0:T(8,128)(2,1)}), bf16[16,16,4224]{2,1,0:T(8,128)(2,1)}, u32[]{:S(2)}, u32[]{:S(2)}) %all-to-all-start.3) | async-done | bytes 2162720 | tf_op jit(solution)/shard_map/all_to_all | solution.py:487
  220.0 12.5 %shard_map.216 = (f32[4096,512]{1,0:T(8,128)}, f32[4096,512]{1,0:T(8,128)}, f32[1]{0:T(128)}) custom-call(f32[4096,512]{1,0:T(8,128)} %copy-done.1, f32[4096,512]{1,0:T(8,128)} %latent_ref.7, bf16[16,16,4224]{2,1,0:T(8,128)(2,1)} %all-to-all-done.3.grad_ref.terms_ref, bf16[16,16,4224]{2,1,0:T(8,128)(2,1)} %all-to-all-done.3.grad_ref.terms_ref, ...), custom_call_target="tpu_custom_call" | custom-call | flops 1073741824 | bytes 35651584 | tf_op jit(solution)/shard_map/pallas_call | solution.py:417
  (2 shorter events, 0.0 us)
Async XLA Ops:
  6.0 6.3 %copy-start.10 = (s32[32]{0:T(128)S(1)}, s32[32]{0:T(128)}, u32[]{:S(2)}) copy-start(s32[32]{0:T(128)} %param.26) | copy-start | bytes 388
  6.0 6.4 %copy-start.8 = (f32[32,65,65]{2,0,1:T(8,128)S(1)}, f32[32,65,65]{2,0,1:T(8,128)}, u32[]{:S(2)}) copy-start(f32[32,65,65]{2,0,1:T(8,128)} %param.25) | copy-start | bytes 1622404
  6.0 54.1 %all-to-all-start = ((bf16[16,16,4096]{2,1,0:T(8,128)(2,1)}), bf16[16,16,4096]{2,1,0:T(8,128)(2,1)}, u32[]{:S(2)}, u32[]{:S(2)}) async-start(bf16[16,16,4096]{2,1,0:T(8,128)(2,1)} %shard_map.210), calls=%async_computation | async-start | bytes 4194304 | tf_op jit(solution)/shard_map/all_to_all | solution.py:482
  12.4 1.9 copy-start.9
  60.0 52.3 %all-to-all-start.2 = ((bf16[16,16,4096]{2,1,0:T(8,128)(2,1)}), bf16[16,16,4096]{2,1,0:T(8,128)(2,1)S(1)}, u32[]{:S(2)}, u32[]{:S(2)}) async-start(bf16[16,16,4096]{2,1,0:T(8,128)(2,1)} %shard_map.214), calls=%async_computation.2 | async-start | bytes 4194304 | tf_op jit(solution)/shard_map/all_to_all | solution.py:482
  112.4 1.4 copy-start.7
  113.7 52.3 %all-to-all-start.1 = ((bf16[16,16,4096]{2,1,0:T(8,128)(2,1)}), bf16[16,16,4096]{2,1,0:T(8,128)(2,1)S(1)}, u32[]{:S(2)}, u32[]{:S(2)}) async-start(bf16[16,16,4096]{2,1,0:T(8,128)(2,1)} %get-tuple-element.21), calls=%async_computation.1 | async-start | bytes 4194304 | tf_op jit(solution)/shard_map/all_to_all | solution.py:487
  166.0 4.8 %copy-start.6 = (s32[4]{0:T(128)S(1)}, s32[4]{0:T(128)}, u32[]{:S(2)}) copy-start(s32[4]{0:T(128)} %select_reduce_fusion.order_ref) | copy-start | bytes 52
  166.0 54.0 %all-to-all-start.3 = ((bf16[16,16,4224]{2,1,0:T(8,128)(2,1)}), bf16[16,16,4224]{2,1,0:T(8,128)(2,1)}, u32[]{:S(2)}, u32[]{:S(2)}) async-start(bf16[16,16,4224]{2,1,0:T(8,128)(2,1)} %get-tuple-element.24), calls=%async_computation.3 | async-start | bytes 4325376 | tf_op jit(solution)/shard_map/all_to_all | solution.py:487
  170.9 1.6 copy-start.4
  172.5 1.6 copy-start.5
  174.1 8.9 %copy-start.3 = (bf16[512,512]{1,0:T(8,128)(2,1)S(1)}, bf16[512,512]{1,0:T(8,128)(2,1)}, u32[]{:S(2)}) copy-start(bf16[512,512]{1,0:T(8,128)(2,1)} %param.23) | copy-start | bytes 1572868
  182.9 3.4 %copy-start = (f32[4096,512]{1,0:T(8,128)S(1)}, f32[4096,512]{1,0:T(8,128)}, u32[]{:S(2)}) copy-start(f32[4096,512]{1,0:T(8,128)} %latent_ref.7) | copy-start | bytes 25165828
  186.3 3.4 %copy-start.2 = (f32[4096,512]{1,0:T(8,128)S(1)}, f32[4096,512]{1,0:T(8,128)}, u32[]{:S(2)}) copy-start(f32[4096,512]{1,0:T(8,128)} %momentum_ref.1) | copy-start | bytes 25165828
  191.6 3.2 %copy-start.1 = (f32[4096,512]{1,0:T(8,128)}, f32[4096,512]{1,0:T(8,128)S(1)}, u32[]{:S(2)}) copy-start(f32[4096,512]{1,0:T(8,128)S(1)} %shard_map.213.kicked_ref) | copy-start | bytes 25165828
